TPU v7x, 32 devices: a whole 2x2x4 slice. The times are simulated.
32 devices in a mesh: row: 8 (over z, core), col: 4 (over y, x).
Axes of the slice: x: 2, y: 2, z: 4, core: 2. Of those that a mesh axis runs over, the one named last changes fastest.
Arguments:
- features: bfloat16 [192, 96, 256], P('row', 'col'), may hold values from -6 to 6
- kernels: bfloat16 [4608, 128], P('row', 'col'), may hold values from -0.125 to 0.125
- out_cotangent: bfloat16 [2, 192, 96, 128], P(None, 'row', 'col'), may hold values from -6 to 6
Outputs:
- branch_maps: bfloat16 [2, 192, 96, 128], P(None, 'row', 'col')
- input_grad: bfloat16 [192, 96, 256], P('row', 'col')
- kernel_grad: float32 [4608, 128], P('row', 'col')
All inputs are finite; a program needn't handle non-finite values.
Results may differ from a plain program's by a relative error of at most 0.001.
Values may be sent and summed in bfloat16 or wider, within the bound.
A program may use at most 64 MiB of HBM per device.

v0:
```python
import jax
import jax.numpy as jnp
from jax import lax
from jax.sharding import PartitionSpec as P

FIRST_SPACING = 12
SECOND_SPACING = 24


def with_halo(x, sides, width):
    for axis, dim in sides:
        size, length = (lax.axis_size(axis), x.shape[dim])
        up = [(i, (i + 1) % size) for i in range(size - 1)]
        down = [(j, i) for i, j in up]
        last = lax.slice_in_dim(x, length - width, length, axis=dim)
        initial = lax.slice_in_dim(x, 0, width, axis=dim)
        before = lax.ppermute(last, axis, up)
        after = lax.ppermute(initial, axis, down)
        x = jnp.concatenate([before, x, after], axis=dim)
    return x


def local(features, kernels, out_cotangent):
    rows_dev = features.shape[0]
    cols_dev = features.shape[1]
    chans = features.shape[2]
    outs_n = out_cotangent.shape[3]
    padding_margin = SECOND_SPACING
    x_ext = with_halo(features, (("row", 0), ("col", 1)), padding_margin)
    g_ext = with_halo(out_cotangent, (("row", 1), ("col", 2)), padding_margin)
    w_cols = lax.all_gather(kernels, "col", axis=1, tiled=True)
    w_full = lax.all_gather(w_cols, "row", axis=0, tiled=True)
    w_blocks = w_full.reshape(2, 9, chans, outs_n)
    pixels = rows_dev * cols_dev
    maps = []
    grads = []
    grad_in = jnp.zeros((pixels, chans), jnp.float32)
    for branch_index, dilation_rate in ((0, FIRST_SPACING), (1, SECOND_SPACING)):
        result = jnp.zeros((pixels, outs_n), jnp.float32)
        g_flat = out_cotangent[branch_index].reshape(pixels, outs_n)
        for kernel_tap in range(9):
            shift_down = (kernel_tap // 3 - 1) * dilation_rate
            shift_across = (kernel_tap % 3 - 1) * dilation_rate
            x_tap = x_ext[
                padding_margin + shift_down : padding_margin + shift_down + rows_dev,
                padding_margin + shift_across : padding_margin + shift_across + cols_dev,
            ].reshape(pixels, chans)
            g_tap = g_ext[
                branch_index,
                padding_margin - shift_down : padding_margin - shift_down + rows_dev,
                padding_margin - shift_across : padding_margin - shift_across + cols_dev,
            ].reshape(pixels, outs_n)
            weight = w_blocks[branch_index, kernel_tap]
            result = result + jnp.dot(x_tap, weight, preferred_element_type=jnp.float32)
            grad_in = grad_in + lax.dot_general(
                g_tap, weight, (((1,), (1,)), ((), ())), preferred_element_type=jnp.float32
            )
            grads.append(
                lax.dot_general(
                    x_tap, g_flat, (((0,), (0,)), ((), ())), preferred_element_type=jnp.float32
                )
            )
        maps.append(result.reshape(rows_dev, cols_dev, outs_n).astype(jnp.bfloat16))
    branch_maps = jnp.stack(maps, 0)
    input_grad = grad_in.reshape(rows_dev, cols_dev, chans).astype(jnp.bfloat16)
    local_grad = jnp.concatenate(grads, 0)
    total_cells = rows_dev * lax.axis_size("row") * cols_dev * lax.axis_size("col")
    scale = 1.0 / jnp.sqrt(jnp.float32(total_cells))
    partial_grad = lax.psum_scatter(local_grad, "row", scatter_dimension=0, tiled=True)
    kernel_grad = lax.psum_scatter(partial_grad, "col", scatter_dimension=1, tiled=True)
    return (branch_maps, input_grad, kernel_grad * scale)


def solution(mesh):
    placed = (P("row", "col", None), P("row", "col"), P(None, "row", "col", None))
    return jax.shard_map(
        local,
        mesh=mesh,
        in_specs=placed,
        out_specs=(P(None, "row", "col", None), P("row", "col", None), P("row", "col")),
        check_vma=False,
    )
```

profile of v0, /device:TPU:0, one launch (start us, length us, event | category | flops | bytes accessed | tf_op | source)
XLA Modules:
  0.0 169.9 jit_solution(2725577153025200455)
XLA Ops:
  7.2 1.4 collective-permute-start.1
  8.7 3.0 %collective-permute-start = (bf16[24,24,256]{2,1,0:T(8,128)(2,1)}, bf16[24,24,256]{2,1,0:T(8,128)(2,1)S(1)}, u32[]{:S(2)}, u32[]{:S(2)}) collective-permute-start(bf16[24,24,256]{2,1,0:T(8,128)(2,1)} %param.3), channel_id=1, source_target_pairs={{0,4},{4,8},{8,12},{12,16},{16,20},{20,24},{24,28},{1,5},{5,9},{9,... | collective-permute-start | bytes 884744 | tf_op jit(solution)/shard_map/ppermute | solution.py:17
  11.7 4.5 %collective-permute-start.4 = (bf16[2,24,24,128]{3,2,1,0:T(8,128)(2,1)}, bf16[2,24,24,128]{3,2,1,0:T(8,128)(2,1)S(1)}, u32[]{:S(2)}, u32[]{:S(2)}) collective-permute-start(bf16[2,24,24,128]{3,2,1,0:T(8,128)(2,1)} %param.5), channel_id=1, source_target_pairs={{0,4},{4,8},{8,12},{12,16},{16,20},{20,24},{24,28},{1,5},{5,9},{9,... | collective-permute-start | bytes 884744 | tf_op jit(solution)/shard_map/ppermute | solution.py:17
  16.3 2.0 %pad_maximum_fusion.6 = (bf16[24,24,256]{2,1,0:T(8,128)(2,1)}, bf16[72,24,256]{2,1,0:T(8,128)(2,1)}, bf16[24,24,256]{2,1,0:T(8,128)(2,1)}) fusion(bf16[24,24,256]{2,1,0:T(8,128)(2,1)} %param.3, bf16[24,24,256]{2,1,0:T(8,128)(2,1)S(1)} %collective-permute-done, bf16[24,24,256]{2,1,0:T(8,128)(2,1)S(1)} %collective-permute-done.1), kind=kLoop, calls=%fused_computation.60 | loop fusion | flops 1179647 | bytes 1769472 | tf_op jit(solution)/shard_map/concatenate | solution.py:19
  18.3 0.8 constant_dynamic-update-slice_fusion.1
  19.1 0.7 constant_dynamic-update-slice_fusion
  19.8 1.3 collective-permute-start.3
  21.1 4.6 %collective-permute-start.2 = (bf16[72,24,256]{2,1,0:T(8,128)(2,1)}, bf16[72,24,256]{2,1,0:T(8,128)(2,1)S(1)}, u32[]{:S(2)}, u32[]{:S(2)}) collective-permute-start(bf16[72,24,256]{2,1,0:T(8,128)(2,1)} %constant_dynamic-update-slice_fusion), channel_id=1, source_target_pairs={{0,1},{1,2},{2,3},{4,5},{5,6},{6,7},{8,9},{9,10},{10,11},{12,13},{... | collective-permute-start | bytes 2654216 | tf_op jit(solution)/shard_map/ppermute | solution.py:17
  25.7 1.3 collective-permute-start.5
  27.0 37.4 %all_gather.6 = bf16[576,128]{0,1:T(8,128)(2,1)S(1)} all-gather(bf16[576,32]{0,1:T(8,128)(2,1)S(1)} %copy-done.47), channel_id=1, replica_groups=mesh['row'=8,'col'=4] {'col'}, dimensions={1}, use_global_device_ids=true | all-gather | bytes 184320 | tf_op jit(solution)/shard_map/all_gather | solution.py:31
  64.5 0.8 copy.9
  65.4 0.8 constant_dynamic-update-slice_fusion.5
  66.1 0.8 constant_dynamic-update-slice_fusion.4
  66.9 0.8 constant_dynamic-update-slice_fusion.3
  67.7 6.1 %collective-permute-start.7 = (bf16[2,72,24,128]{3,2,1,0:T(8,128)(2,1)}, bf16[2,72,24,128]{3,2,1,0:T(8,128)(2,1)}, u32[]{:S(2)}, u32[]{:S(2)}) collective-permute-start(bf16[2,72,24,128]{3,2,1,0:T(8,128)(2,1)} %constant_dynamic-update-slice_fusion.3), channel_id=1, source_target_pairs={{0,1},{1,2},{2,3},{4,5},{5,6},{6,7},{8,9},{9,10},{10,11},{12,13},{... | collective-permute-start | bytes 2654216 | tf_op jit(solution)/shard_map/ppermute | solution.py:17
  73.8 1.3 collective-permute-start.6
  75.1 0.8 pad_maximum_fusion.15
  75.9 2.4 %pad_maximum_fusion.3 = (bf16[24,24,256]{2,1,0:T(8,128)(2,1)S(1)}, bf16[24,24,256]{2,1,0:T(8,128)(2,1)S(1)}, bf16[24,24,256]{2,1,0:T(8,128)(2,1)S(1)}, bf16[24,2...) fusion(bf16[72,24,256]{2,1,0:T(8,128)(2,1)S(1)} %collective-per, ...), kind=kLoop, calls=%fused_computation.57 | loop fusion | flops 3538944 | bytes 7962624 | tf_op jit(solution)/shard_map/slice | solution.py:44
  78.4 1.3 convolution_dynamic-update-slice_fusion.17
  79.8 1.0 convolution_dynamic-update-slice_fusion.16
  80.7 0.9 convolution_dynamic-update-slice_fusion.15
  81.7 0.9 convolution_dynamic-update-slice_fusion.14
  82.6 0.9 convolution_dynamic-update-slice_fusion.13
  83.6 0.9 convolution_dynamic-update-slice_fusion.12
  84.5 0.9 convolution_dynamic-update-slice_fusion.11
  85.5 1.0 convolution_dynamic-update-slice_fusion.10
  86.4 1.0 convolution_dynamic-update-slice_fusion.9
  87.4 0.9 convolution_dynamic-update-slice_fusion.8
  88.3 0.9 convolution_dynamic-update-slice_fusion.7
  89.3 1.0 convolution_dynamic-update-slice_fusion.6
  90.2 0.9 convolution_dynamic-update-slice_fusion.5
  91.2 1.0 convolution_dynamic-update-slice_fusion.4
  92.1 0.9 convolution_dynamic-update-slice_fusion.3
  93.1 1.0 convolution_dynamic-update-slice_fusion.2
  94.0 0.9 convolution_dynamic-update-slice_fusion.1
  95.0 0.9 convolution_dynamic-update-slice_fusion
  96.0 17.6 %collective-permute-done.6 = bf16[2,72,24,128]{3,2,1,0:T(8,128)(2,1)} collective-permute-done((bf16[2,72,24,128]{3,2,1,0:T(8,128)(2,1)}, bf16[2,72,24,128]{3,2,1,0:T(8,128)(2,1)}, u32[]{:S(2)}, u32[]{:S(2)}) %collective-permute-start.6) | collective-permute-done | bytes 884768 | tf_op jit(solution)/shard_map/ppermute | solution.py:18
  113.6 2.9 %pad_maximum_fusion.12 = (bf16[1,24,24,128]{3,2,1,0:T(8,128)(2,1)}, bf16[1,24,24,128]{3,2,1,0:T(8,128)(2,1)}, bf16[1,24,24,128]{3,2,1,0:T(8,128)(2,1)}, bf16[1,2...) fusion(bf16[2,72,24,128]{3,2,1,0:T(8,128)(2,1)} %constant_dynam, ...), kind=kLoop, calls=%fused_computation.66 | loop fusion | flops 1769472 | bytes 5308416 | tf_op jit(solution)/shard_map/slice | solution.py:48
  116.5 1.2 fusion.51
  117.7 1.1 fusion.36
  119.2 0.2 fusion.35
  119.7 0.2 copy-done.26
  120.7 0.3 copy-done.19
  123.4 1.1 fusion.54
  125.0 0.2 fusion.41
  125.9 1.0 fusion.52
  127.2 0.2 fusion.43
  127.5 0.2 fusion.46
  128.0 0.3 fusion.26
  128.2 0.3 copy-done.3
  128.5 0.9 fusion.27
  129.4 0.3 fusion.24
  129.7 0.3 fusion.28
  129.9 0.6 copy-done.37
  130.6 0.2 fusion.2
  130.8 0.7 copy-done.36
  131.5 0.4 fusion.10
  131.9 3.4 %reduce-scatter.5.cloned.1.call-done = f32[576,128]{1,0:T(8,128)} async-done(((f32[4608,128]{1,0:T(8,128)}), f32[576,128]{1,0:T(8,128)}) %reduce-scatter.5.cloned.1.call-update) | async-done | bytes 294928 | tf_op jit(solution)/shard_map/reduce_scatter | solution.py:69
  135.3 1.9 %copy.11 = f32[576,128]{0,1:T(8,128)} copy(f32[576,128]{1,0:T(8,128)} %reduce-scatter.5.cloned.1.call-done) | data formatting | bytes 589824
  137.2 0.7 pad_maximum_fusion.8
  138.2 1.0 fusion.14
  139.2 22.3 %reduce-scatter.7.cloned.1.call-done = f32[32,576]{1,0:T(8,128)} async-done(((f32[128,576]{1,0:T(8,128)}), f32[32,576]{1,0:T(8,128)}) %reduce-scatter.7.cloned.1.call-update) | async-done | bytes 73744
  161.6 1.0 copy.12
  162.6 0.8 copy.10
  (127 shorter events, 5.8 us)
Async XLA Ops:
  7.2 11.2 %copy-start = (bf16[24,24,256]{2,1,0:T(8,128)(2,1)S(1)}, bf16[24,24,256]{2,1,0:T(8,128)(2,1)}, u32[]{:S(2)}) copy-start(bf16[24,24,256]{2,1,0:T(8,128)(2,1)} %param.3) | copy-start | bytes 884740
  7.2 18.6 %copy-start.27 = (bf16[2,24,24,128]{3,2,1,0:T(8,128)(2,1)S(1)}, bf16[2,24,24,128]{3,2,1,0:T(8,128)(2,1)}, u32[]{:S(2)}) copy-start(bf16[2,24,24,128]{3,2,1,0:T(8,128)(2,1)} %param.5) | copy-start | bytes 884740
  7.2 19.9 %copy-start.47 = (bf16[576,32]{0,1:T(8,128)(2,1)S(1)}, bf16[576,32]{0,1:T(8,128)(2,1)}, u32[]{:S(2)}) copy-start(bf16[576,32]{0,1:T(8,128)(2,1)} %param.4) | copy-start | bytes 110596
  7.2 109.3 %all-gather.2.cloned.1.call-start = ((), (), s32[]{:S(2)}) async-start(), calls=%async_computation.2 | async-start | bytes 1327104 | tf_op jit(solution)/shard_map/all_gather | solution.py:32
  7.2 9.0 %collective-permute-start.1 = (bf16[24,24,256]{2,1,0:T(8,128)(2,1)}, bf16[24,24,256]{2,1,0:T(8,128)(2,1)S(1)}, u32[]{:S(2)}, u32[]{:S(2)}) collective-permute-start(bf16[24,24,256]{2,1,0:T(8,128)(2,1)} %param.3), channel_id=1, source_target_pairs={{4,0},{8,4},{12,8},{16,12},{20,16},{24,20},{28,24},{5,1},{9,5},{13... | collective-permute-start | bytes 884744 | tf_op jit(solution)/shard_map/ppermute | solution.py:18
  8.7 7.6 %collective-permute-start = (bf16[24,24,256]{2,1,0:T(8,128)(2,1)}, bf16[24,24,256]{2,1,0:T(8,128)(2,1)S(1)}, u32[]{:S(2)}, u32[]{:S(2)}) collective-permute-start(bf16[24,24,256]{2,1,0:T(8,128)(2,1)} %param.3), channel_id=1, source_target_pairs={{0,4},{4,8},{8,12},{12,16},{16,20},{20,24},{24,28},{1,5},{5,9},{9,... | collective-permute-start | bytes 884744 | tf_op jit(solution)/shard_map/ppermute | solution.py:17
  11.7 53.6 %collective-permute-start.4 = (bf16[2,24,24,128]{3,2,1,0:T(8,128)(2,1)}, bf16[2,24,24,128]{3,2,1,0:T(8,128)(2,1)S(1)}, u32[]{:S(2)}, u32[]{:S(2)}) collective-permute-start(bf16[2,24,24,128]{3,2,1,0:T(8,128)(2,1)} %param.5), channel_id=1, source_target_pairs={{0,4},{4,8},{8,12},{12,16},{16,20},{20,24},{24,28},{1,5},{5,9},{9,... | collective-permute-start | bytes 884744 | tf_op jit(solution)/shard_map/ppermute | solution.py:17
  16.3 2.8 %copy-start.22 = (bf16[24,24,256]{2,1,0:T(8,128)(2,1)}, bf16[24,24,256]{2,1,0:T(8,128)(2,1)S(1)}, u32[]{:S(2)}) copy-start(bf16[24,24,256]{2,1,0:T(8,128)(2,1)S(1)} %collective-permute-done) | copy-start | bytes 884740
  19.8 56.1 %collective-permute-start.3 = (bf16[72,24,256]{2,1,0:T(8,128)(2,1)}, bf16[72,24,256]{2,1,0:T(8,128)(2,1)S(1)}, u32[]{:S(2)}, u32[]{:S(2)}) collective-permute-start(bf16[72,24,256]{2,1,0:T(8,128)(2,1)} %constant_dynamic-update-slice_fusion), channel_id=1, source_target_pairs={{1,0},{2,1},{3,2},{5,4},{6,5},{7,6},{9,8},{10,9},{11,10},{13,12},{... | collective-permute-start | bytes 2654216 | tf_op jit(solution)/shard_map/ppermute | solution.py:18
  21.1 54.8 %collective-permute-start.2 = (bf16[72,24,256]{2,1,0:T(8,128)(2,1)}, bf16[72,24,256]{2,1,0:T(8,128)(2,1)S(1)}, u32[]{:S(2)}, u32[]{:S(2)}) collective-permute-start(bf16[72,24,256]{2,1,0:T(8,128)(2,1)} %constant_dynamic-update-slice_fusion), channel_id=1, source_target_pairs={{0,1},{1,2},{2,3},{4,5},{5,6},{6,7},{8,9},{9,10},{10,11},{12,13},{... | collective-permute-start | bytes 2654216 | tf_op jit(solution)/shard_map/ppermute | solution.py:17
  25.7 41.2 %collective-permute-start.5 = (bf16[2,24,24,128]{3,2,1,0:T(8,128)(2,1)S(1)}, bf16[2,24,24,128]{3,2,1,0:T(8,128)(2,1)S(1)}, u32[]{:S(2)}, u32[]{:S(2)}) collective-permute-start(bf16[2,24,24,128]{3,2,1,0:T(8,128)(2,1)S(1)} %copy-done.27), channel_id=1, source_target_pairs={{4,0},{8,4},{12,8},{16,12},{20,16},{24,20},{28,24},{5,1},{9,5},{13... | collective-permute-start | bytes 884744 | tf_op jit(solution)/shard_map/ppermute | solution.py:18
  65.3 70.0 %reduce-scatter.5.cloned.1.call-start = ((), (), s32[]{:S(2)}) async-start(), calls=%async_computation.3 | async-start | bytes 2654208 | tf_op jit(solution)/shard_map/reduce_scatter | solution.py:69
  67.7 28.3 %collective-permute-start.7 = (bf16[2,72,24,128]{3,2,1,0:T(8,128)(2,1)}, bf16[2,72,24,128]{3,2,1,0:T(8,128)(2,1)}, u32[]{:S(2)}, u32[]{:S(2)}) collective-permute-start(bf16[2,72,24,128]{3,2,1,0:T(8,128)(2,1)} %constant_dynamic-update-slice_fusion.3), channel_id=1, source_target_pairs={{0,1},{1,2},{2,3},{4,5},{5,6},{6,7},{8,9},{9,10},{10,11},{12,13},{... | collective-permute-start | bytes 2654216 | tf_op jit(solution)/shard_map/ppermute | solution.py:17
  73.8 39.8 %collective-permute-start.6 = (bf16[2,72,24,128]{3,2,1,0:T(8,128)(2,1)}, bf16[2,72,24,128]{3,2,1,0:T(8,128)(2,1)}, u32[]{:S(2)}, u32[]{:S(2)}) collective-permute-start(bf16[2,72,24,128]{3,2,1,0:T(8,128)(2,1)} %constant_dynamic-update-slice_fusion.3), channel_id=1, source_target_pairs={{1,0},{2,1},{3,2},{5,4},{6,5},{7,6},{9,8},{10,9},{11,10},{13,12},{... | collective-permute-start | bytes 2654216 | tf_op jit(solution)/shard_map/ppermute | solution.py:18
  75.9 3.8 %copy-start.25 = (bf16[24,24,256]{2,1,0:T(8,128)(2,1)S(1)}, bf16[24,24,256]{2,1,0:T(8,128)(2,1)}, u32[]{:S(2)}) copy-start(bf16[24,24,256]{2,1,0:T(8,128)(2,1)} %get-tuple-element.48) | copy-start | bytes 884740
  78.3 5.2 %copy-start.4 = (bf16[24,24,256]{2,1,0:T(8,128)(2,1)}, bf16[24,24,256]{2,1,0:T(8,128)(2,1)S(1)}, u32[]{:S(2)}) copy-start(bf16[24,24,256]{2,1,0:T(8,128)(2,1)S(1)} %get-tuple-element.35) | copy-start | bytes 884740
  78.3 5.2 %copy-start.14 = (bf16[24,24,256]{2,1,0:T(8,128)(2,1)}, bf16[24,24,256]{2,1,0:T(8,128)(2,1)S(1)}, u32[]{:S(2)}) copy-start(bf16[24,24,256]{2,1,0:T(8,128)(2,1)S(1)} %get-tuple-element.34) | copy-start | bytes 884740
  78.3 5.2 %copy-start.2 = (bf16[24,24,256]{2,1,0:T(8,128)(2,1)}, bf16[24,24,256]{2,1,0:T(8,128)(2,1)S(1)}, u32[]{:S(2)}) copy-start(bf16[24,24,256]{2,1,0:T(8,128)(2,1)S(1)} %get-tuple-element.18) | copy-start | bytes 884740
  78.4 6.2 %copy-start.16 = (bf16[24,24,256]{2,1,0:T(8,128)(2,1)}, bf16[24,24,256]{2,1,0:T(8,128)(2,1)S(1)}, u32[]{:S(2)}) copy-start(bf16[24,24,256]{2,1,0:T(8,128)(2,1)S(1)} %get-tuple-element.33) | copy-start | bytes 884740
  78.4 8.1 %copy-start.18 = (bf16[24,24,256]{2,1,0:T(8,128)(2,1)}, bf16[24,24,256]{2,1,0:T(8,128)(2,1)S(1)}, u32[]{:S(2)}) copy-start(bf16[24,24,256]{2,1,0:T(8,128)(2,1)S(1)} %get-tuple-element.20) | copy-start | bytes 884740
  78.4 10.9 %copy-start.6 = (bf16[24,24,256]{2,1,0:T(8,128)(2,1)}, bf16[24,24,256]{2,1,0:T(8,128)(2,1)S(1)}, u32[]{:S(2)}) copy-start(bf16[24,24,256]{2,1,0:T(8,128)(2,1)S(1)} %get-tuple-element.41) | copy-start | bytes 884740
  78.4 11.8 %copy-start.10 = (bf16[24,24,256]{2,1,0:T(8,128)(2,1)}, bf16[24,24,256]{2,1,0:T(8,128)(2,1)S(1)}, u32[]{:S(2)}) copy-start(bf16[24,24,256]{2,1,0:T(8,128)(2,1)S(1)} %get-tuple-element.37) | copy-start | bytes 884740
  78.4 12.8 %copy-start.20 = (bf16[24,24,256]{2,1,0:T(8,128)(2,1)}, bf16[24,24,256]{2,1,0:T(8,128)(2,1)S(1)}, u32[]{:S(2)}) copy-start(bf16[24,24,256]{2,1,0:T(8,128)(2,1)S(1)} %get-tuple-element.19) | copy-start | bytes 884740
  78.4 14.7 %copy-start.12 = (bf16[24,24,256]{2,1,0:T(8,128)(2,1)}, bf16[24,24,256]{2,1,0:T(8,128)(2,1)S(1)}, u32[]{:S(2)}) copy-start(bf16[24,24,256]{2,1,0:T(8,128)(2,1)S(1)} %get-tuple-element.36) | copy-start | bytes 884740
  78.4 16.5 %copy-start.8 = (bf16[24,24,256]{2,1,0:T(8,128)(2,1)}, bf16[24,24,256]{2,1,0:T(8,128)(2,1)S(1)}, u32[]{:S(2)}) copy-start(bf16[24,24,256]{2,1,0:T(8,128)(2,1)S(1)} %get-tuple-element.39) | copy-start | bytes 884740
  81.7 3.8 %copy-start.24 = (bf16[24,24,256]{2,1,0:T(8,128)(2,1)S(1)}, bf16[24,24,256]{2,1,0:T(8,128)(2,1)}, u32[]{:S(2)}) copy-start(bf16[24,24,256]{2,1,0:T(8,128)(2,1)} %get-tuple-element.50) | copy-start | bytes 884740
  84.5 3.8 %copy-start.23 = (bf16[24,24,256]{2,1,0:T(8,128)(2,1)S(1)}, bf16[24,24,256]{2,1,0:T(8,128)(2,1)}, u32[]{:S(2)}) copy-start(bf16[24,24,256]{2,1,0:T(8,128)(2,1)} %copy-done.22) | copy-start | bytes 884740
  95.9 65.6 %reduce-scatter.7.cloned.1.call-start = ((), (), s32[]{:S(2)}) async-start(), calls=%async_computation.4 | async-start | bytes 409600
  116.5 2.3 %copy-start.1 = (bf16[4608,128]{1,0:T(8,128)(2,1)S(1)}, bf16[4608,128]{1,0:T(8,128)(2,1)}, u32[]{:S(2)}) copy-start(bf16[4608,128]{1,0:T(8,128)(2,1)} %all-gather.2.cloned.1.call-done) | copy-start | bytes 3538948
  119.0 1.0 copy-start.26
  119.5 1.0 copy-start.21
  120.0 1.0 copy-start.19
  120.0 1.2 copy-start.17
  120.2 1.2 copy-start.15
  120.5 1.2 copy-start.13
  121.0 1.0 copy-start.11
  121.2 1.0 copy-start.9
  121.4 1.0 copy-start.7
  121.7 1.0 copy-start.33
  122.2 0.9 copy-start.32
  122.5 0.9 copy-start.31
  122.7 1.8 %copy-start.30 = (bf16[1,24,24,128]{3,2,1,0:T(8,128)(2,1)S(1)}, bf16[1,24,24,128]{3,2,1,0:T(8,128)(2,1)}, u32[]{:S(2)}) copy-start(bf16[1,24,24,128]{3,2,1,0:T(8,128)(2,1)} %get-tuple-element.47) | copy-start | bytes 442372
  123.2 1.6 copy-start.46
  123.4 1.6 copy-start.45
  124.5 0.9 copy-start.44
  124.7 0.9 copy-start.43
  125.0 0.9 copy-start.42
  125.4 1.6 copy-start.41
  125.7 1.6 copy-start.40
  125.9 1.5 copy-start.39
  127.0 1.0 copy-start.5
  127.5 1.0 copy-start.3
  129.6 0.9 copy-start.37
  130.6 0.9 copy-start.36
  131.5 5.8 %copy-start.34 = (bf16[576,128]{1,0:T(8,128)(2,1)S(1)}, bf16[576,128]{1,0:T(8,128)(2,1)}, u32[]{:S(2)}) copy-start(bf16[576,128]{1,0:T(8,128)(2,1)} %fusion.27) | copy-start | bytes 442372
  131.9 6.1 %copy-start.38 = (bf16[1,24,24,128]{3,2,1,0:T(8,128)(2,1)S(1)}, bf16[1,24,24,128]{3,2,1,0:T(8,128)(2,1)}, u32[]{:S(2)}) copy-start(bf16[1,24,24,128]{3,2,1,0:T(8,128)(2,1)} %get-tuple-element.31) | copy-start | bytes 442372
  131.9 6.3 %copy-start.28 = (f32[576,256]{1,0:T(8,128)S(1)}, f32[576,256]{1,0:T(8,128)}, u32[]{:S(2)}) copy-start(f32[576,256]{1,0:T(8,128)} %fusion.54) | copy-start | bytes 1769476
  131.9 6.3 %copy-start.29 = (f32[576,256]{1,0:T(8,128)S(1)}, f32[576,256]{1,0:T(8,128)}, u32[]{:S(2)}) copy-start(f32[576,256]{1,0:T(8,128)} %fusion.52) | copy-start | bytes 1769476
  131.9 6.3 %copy-start.35 = (bf16[1,24,24,128]{3,2,1,0:T(8,128)(2,1)S(1)}, bf16[1,24,24,128]{3,2,1,0:T(8,128)(2,1)}, u32[]{:S(2)}) copy-start(bf16[1,24,24,128]{3,2,1,0:T(8,128)(2,1)} %get-tuple-element.24) | copy-start | bytes 442372
Sparse Core Ops, SparseCore 0:
  65.4 26.3 all-gather.1
  96.1 39.2 reduce-scatter.4
  138.1 23.4 reduce-scatter.6
where the time goes:
time: 171 us; the launch traced here: 170 us
  waiting for transfers between devices  43.4 us (25%)
  blocking collectives  37.4 us (22%)
  matrix products  30.7 us (18%)
  starting transfers between devices  23.7 us (14%)
  between operations  14.5 us (8%)
  local copies, waits for them, and re-layouts  11.2 us (7%)
  other arithmetic  8.92 us (5%)
    all_gather x1, blocking collectives, local(): w_cols = lax.all_gather(kernels, 'col', axis=1, tiled=True)  37.4 us
    unnamed x4, waiting for transfers between devices  22.4 us
    ppermute x4, starting transfers between devices, with_halo(): before = lax.ppermute(last, axis, up)  18.3 us
    ppermute x4, waiting for transfers between devices, with_halo(): after = lax.ppermute(initial, axis, down)  17.6 us
    dot_general x18, matrix products, local(): lax.dot_general(x_tap, g_flat, (((0,), (0,)), ((), ())), preferred_elemen...  17.4 us
    unnamed x102, local copies, waits for them, and re-layouts  8.93 us
    dot_general x18, matrix products, local(): lax.dot_general(g_tap, weight, (((1,), (1,)), ((), ())), preferred_elemen...  6.7 us
    dot_general x18, matrix products, local(): result = result + jnp.dot(x_tap, weight, preferred_element_type=jnp.float32)  6.55 us
  transfers between devices with their start and end apart: 11, of which 3 were waited for; matrix products, arithmetic and copies ran while one was open for 26% of the time, Pallas kernels for 0%

commit v1 on v0

--- a/solution.py
+++ b/solution.py
@@ -1,10 +1,382 @@
+import functools
+
 import jax
 import jax.numpy as jnp
 from jax import lax
+from jax.experimental import pallas as pl
+from jax.experimental.pallas import tpu as pltpu
 from jax.sharding import PartitionSpec as P
 
 FIRST_SPACING = 12
 SECOND_SPACING = 24
+UNITS = 36
+PIECE = 36
+SLOT = 48
+MESH = pl.DeviceIdType.MESH
+
+
+def kernel(n_row, n_col, scale, gs_ref, xs_ref, ks_ref, om_ref, oi_ref, ok_ref,
+           ga, xa, gp, xp, kb, k2, ru, ra, sb, rb_, tc, rc, fin, fx, macc, iacc, ms, igs,
+           a_send, a_recv, h_send, h_recv, k_send, k_recv, o_send, o_recv, r_send, r_recv):
+    nz = n_row // 2
+    per_z = UNITS // nz
+    r = lax.axis_index("row")
+    j = lax.axis_index("col")
+    z = r // 2
+    c = r % 2
+    sib = r + 1 - 2 * c
+    cols = [lax.rem(j + i, n_col) for i in range(1, n_col)]
+    zs = [lax.rem(z + i, nz) for i in range(1, nz)]
+    far = r - 1 + 2 * c
+    has_up = r > 0
+    has_down = r < n_row - 1
+    has_far = jnp.where(c == 0, has_up, has_down)
+
+    barrier = pltpu.get_barrier_semaphore()
+    for s in cols:
+        pl.semaphore_signal(barrier, inc=1, device_id={"col": s}, device_id_type=MESH)
+    for zz in zs:
+        pl.semaphore_signal(barrier, inc=1, device_id={"row": zz * 2 + c}, device_id_type=MESH)
+    pl.semaphore_signal(barrier, inc=1, device_id={"row": sib}, device_id_type=MESH)
+
+    @pl.when(has_far)
+    def _():
+        pl.semaphore_signal(barrier, inc=1, device_id={"row": far}, device_id_type=MESH)
+
+    pl.semaphore_wait(barrier, n_col - 1 + nz - 1 + 1 + jnp.where(has_far, 1, 0))
+
+    def remote(src, dst, ssem, rsem, dev):
+        return pltpu.make_async_remote_copy(
+            src_ref=src, dst_ref=dst, send_sem=ssem, recv_sem=rsem,
+            device_id=dev, device_id_type=MESH)
+
+    arrays = ((gs_ref, ga), (xs_ref, xa))
+    sends = []
+    for a, (src, dst) in enumerate(arrays):
+        for s in cols:
+            cp = remote(src.at[s], dst.at[1, j], a_send.at[a, s], a_recv.at[a, j], {"col": s})
+            cp.start()
+            sends.append(cp)
+        if a == 0:
+            for zz in zs:
+                cp = remote(ks_ref, kb.at[c, j, z], k_send.at[0, zz], k_recv.at[0, z], {"row": zz * 2 + c})
+                cp.start()
+                sends.append(cp)
+    kb[c, j, z] = ks_ref[...]
+    for src, dst in arrays:
+        dst[1, j] = src[j]
+    gp[...] = jnp.zeros_like(gp)
+    xp[...] = jnp.zeros_like(xp)
+
+    def halo(a, s, up):
+        buf = arrays[a][1]
+        to = r - 1 if up else r + 1
+        d = 0 if up else 1
+        return remote(buf.at[1, s], buf.at[2 if up else 0, s],
+                      h_send.at[a, d, s], h_recv.at[a, d, s], {"row": to})
+
+    def spread(a, s):
+        @pl.when(has_up)
+        def _():
+            halo(a, s, True).start()
+
+        @pl.when(has_down)
+        def _():
+            halo(a, s, False).start()
+
+    def gather(a):
+        src, dst = arrays[a]
+        spread(a, j)
+        for i in range(1, n_col):
+            s = lax.rem(j + n_col - i, n_col)
+            remote(src.at[s], dst.at[1, s], a_send.at[a, s], a_recv.at[a, s], {"col": s}).wait_recv()
+            spread(a, s)
+
+    def halo_wait(a):
+        for s in range(n_col):
+            @pl.when(has_down)
+            def _():
+                halo(a, s, True).wait_recv()
+
+            @pl.when(has_up)
+            def _():
+                halo(a, s, False).wait_recv()
+
+    def halo_done(a):
+        for s in range(n_col):
+            @pl.when(has_up)
+            def _():
+                halo(a, s, True).wait_send()
+
+            @pl.when(has_down)
+            def _():
+                halo(a, s, False).wait_send()
+
+    gather(0)
+    for i in range(1, nz):
+        zz = lax.rem(z + nz - i, nz)
+        remote(ks_ref, kb.at[c, j, zz], k_send.at[0, zz], k_recv.at[0, zz], {"row": zz * 2 + c}).wait_recv()
+    for s in cols:
+        cp = remote(kb.at[c, j], kb.at[c, j], k_send.at[1, s], k_recv.at[1, j], {"col": s})
+        cp.start()
+        sends.append(cp)
+    gather(1)
+
+    def place(n):
+        for s in range(n_col):
+            for b in range(2):
+                block = ga[n, s, b].astype(jnp.float32)
+                for m in range(4):
+                    part = block[PIECE * m : PIECE * (m + 1)].astype(jnp.bfloat16)
+                    gp[b, 2 * n + m // 2, 2 + 2 * s + m % 2, 0:PIECE, :] = part
+
+    def place_x(n):
+        for s in range(n_col):
+            block = xa[n, s].astype(jnp.float32)
+            for m in range(4):
+                part = block[PIECE * m : PIECE * (m + 1)].astype(jnp.bfloat16)
+                xp[2 * n + m // 2, 2 + 2 * s + m % 2, 0:PIECE, :] = part
+
+    place(1)
+    place_x(1)
+    halo_wait(0)
+
+    @pl.when(has_up)
+    def _():
+        place(0)
+
+    @pl.when(has_down)
+    def _():
+        place(2)
+
+    qs = 2 * n_col
+    pix = 2 * qs * SLOT
+
+    def g_tap(b, t):
+        d = 1 + b
+        sy = (t // 3 - 1) * d
+        sx = (t % 3 - 1) * d
+        return gp[b, pl.ds(2 - sy, 2), pl.ds(2 - sx, qs)].reshape(pix, gp.shape[-1])
+
+    def x_tap(b, t):
+        d = 1 + b
+        sy = (t // 3 - 1) * d
+        sx = (t % 3 - 1) * d
+        return xp[pl.ds(2 + sy, 2), pl.ds(2 + sx, qs)].reshape(pix, xp.shape[-1])
+
+    outs_n = gp.shape[-1]
+    per_col = outs_n // n_col
+    half = per_col // 2
+
+    def pair(b):
+        us = pl.ds(18 * b, 18)
+        return remote(ru.at[us, :, 1 - c], ra.at[us], r_send.at[0, b], r_recv.at[0, b], {"row": sib})
+
+    for b in (1, 0):
+        def body(t, carry):
+            x_here = xp[pl.ds(2, 2), pl.ds(2, qs)].reshape(pix, xp.shape[-1])
+            res = lax.dot_general(g_tap(b, t), x_here, (((0,), (0,)), ((), ())),
+                                  preferred_element_type=jnp.float32)
+            for h in range(2):
+                ru[2 * (9 * b + t) + h] = res[:, 128 * h : 128 * (h + 1)].reshape(n_col, 2, half, 128)
+            return carry
+
+        lax.fori_loop(0, 9, body, 0)
+        pair(b).start()
+
+    for i in range(1, n_col):
+        s = lax.rem(j + n_col - i, n_col)
+        remote(kb.at[c, s], kb.at[c, s], k_send.at[1, s], k_recv.at[1, s], {"col": s}).wait_recv()
+    swap = remote(kb.at[c], kb.at[c], k_send.at[2, 0], k_recv.at[2, 0], {"row": sib})
+    swap.start()
+    sends.append(swap)
+
+    def plane(b, s):
+        us = pl.ds(18 * b, 18)
+        return remote(sb.at[s, us], rb_.at[j, us], r_send.at[1 + b, s], r_recv.at[1 + b, j], {"col": s})
+
+    for b in (1, 0):
+        us = pl.ds(18 * b, 18)
+        pair(b).wait_recv()
+        for s in range(n_col):
+            sb[s, us] = ru[us, s, c] + ra[us, s]
+        for s in cols:
+            plane(b, s).start()
+
+    remote(kb.at[1 - c], kb.at[1 - c], k_send.at[2, 0], k_recv.at[2, 0], {"row": sib}).wait_recv()
+    for u in range(UNITS):
+        zz, v = divmod(u, per_z)
+        mid = per_z // 2
+        if v < mid:
+            val = kb[0, :, zz, v]
+        elif v > mid:
+            val = kb[1, :, zz, v - mid]
+        else:
+            val = kb[0, :, zz, mid] + kb[1, :, zz, 0]
+        k2[u // 2, :, 128 * (u % 2) : 128 * (u % 2 + 1)] = val.reshape(outs_n, 128)
+
+    halo_wait(1)
+
+    @pl.when(has_up)
+    def _():
+        place_x(0)
+
+    @pl.when(has_down)
+    def _():
+        place_x(2)
+
+    def pack(acc, s):
+        parts = []
+        for m in range(4):
+            p = ((m // 2) * qs + 2 * s + m % 2) * SLOT
+            parts.append(acc[p : p + PIECE])
+        return jnp.concatenate(parts, axis=0).astype(jnp.bfloat16)
+
+    def back(k, s):
+        src = ms if k == 0 else igs
+        dst = om_ref if k == 0 else oi_ref
+        return remote(src.at[s], dst.at[j], o_send.at[k, s], o_recv.at[k, j], {"col": s})
+
+    iacc[...] = jnp.zeros_like(iacc)
+    for b in range(2):
+        def body(t, carry):
+            iacc[...] += jnp.dot(g_tap(b, t), k2[9 * b + t], preferred_element_type=jnp.float32)
+            return carry
+
+        lax.fori_loop(0, 9, body, 0)
+    for s in range(n_col):
+        igs[s] = pack(iacc, s)
+    for s in cols:
+        back(1, s).start()
+    oi_ref[j] = igs[j]
+
+    for b in range(2):
+        macc[...] = jnp.zeros_like(macc)
+
+        def body(t, carry):
+            macc[...] += lax.dot_general(x_tap(b, t), k2[9 * b + t], (((1,), (1,)), ((), ())),
+                                         preferred_element_type=jnp.float32)
+            return carry
+
+        lax.fori_loop(0, 9, body, 0)
+        for s in range(n_col):
+            ms[s, b] = pack(macc, s)
+    for s in cols:
+        back(0, s).start()
+    om_ref[j] = ms[j]
+
+    for b in (1, 0):
+        us = pl.ds(18 * b, 18)
+        total = sb[j, us]
+        for i in range(1, n_col):
+            s = lax.rem(j + n_col - i, n_col)
+            remote(sb.at[s, us], rb_.at[s, us], r_send.at[1 + b, s], r_recv.at[1 + b, s], {"col": s}).wait_recv()
+            total = total + rb_[s, us]
+        tc[us] = total
+    for zz in zs:
+        cp = remote(tc.at[pl.ds(zz * per_z, per_z)], rc.at[z], r_send.at[3, zz], r_recv.at[3, z],
+                    {"row": zz * 2 + c})
+        cp.start()
+        sends.append(cp)
+    mine = tc[pl.ds(z * per_z, per_z)]
+    for i in range(1, nz):
+        zz = lax.rem(z + nz - i, nz)
+        remote(tc.at[pl.ds(zz * per_z, per_z)], rc.at[zz], r_send.at[3, zz], r_recv.at[3, zz],
+               {"row": zz * 2 + c}).wait_recv()
+        mine = mine + rc[zz]
+    fin[...] = mine * scale
+    last = remote(fin, fx, r_send.at[4, 0], r_recv.at[4, 0], {"row": sib})
+    last.start()
+    ok_ref[:, c] = fin[...]
+    last.wait()
+    ok_ref[:, 1 - c] = fx[...]
+
+    for k in range(2):
+        for i in range(1, n_col):
+            s = lax.rem(j + n_col - i, n_col)
+            src = ms if k == 0 else igs
+            dst = om_ref if k == 0 else oi_ref
+            remote(src.at[s], dst.at[s], o_send.at[k, s], o_recv.at[k, s], {"col": s}).wait_recv()
+        for s in cols:
+            back(k, s).wait_send()
+    for b in (1, 0):
+        pair(b).wait_send()
+        for s in cols:
+            plane(b, s).wait_send()
+    for cp in sends:
+        cp.wait_send()
+    halo_done(0)
+    halo_done(1)
+
+
+def phased(n_row, n_col, features, kernels, out_cotangent):
+    nz = n_row // 2
+    per_z = UNITS // nz
+    chans = features.shape[2]
+    outs_n = out_cotangent.shape[3]
+    kk = 12 // n_col
+    per_col = outs_n // n_col
+    c = lax.axis_index("row") % 2
+    bf, f32 = jnp.bfloat16, jnp.float32
+    xs = features.reshape(2, 12, 2, n_col, kk, chans).transpose(3, 0, 2, 1, 4, 5)
+    xs = xs.reshape(n_col, 4 * PIECE, chans)
+    gs = out_cotangent.reshape(2, 2, 12, 2, n_col, kk, outs_n).transpose(4, 0, 1, 3, 2, 5, 6)
+    gs = gs.reshape(n_col, 2, 4 * PIECE, outs_n)
+    kt = kernels.T
+    kt = jnp.where(c == 0, jnp.pad(kt, ((0, 0), (0, 64))), jnp.pad(kt, ((0, 0), (64, 0))))
+    held = (per_z + 1) // 2
+    ks = kt.reshape(per_col, held, 128).transpose(1, 0, 2)
+    cells = features.shape[0] * n_row * features.shape[1] * n_col
+    scale = 1.0 / float(cells) ** 0.5
+    qs = 2 * n_col
+    pix = 2 * qs * SLOT
+    half = per_col // 2
+    vm = pl.BlockSpec(memory_space=pltpu.VMEM)
+    dma = pltpu.SemaphoreType.DMA
+    om, oi, ok = pl.pallas_call(
+        functools.partial(kernel, n_row, n_col, scale),
+        out_shape=(
+            jax.ShapeDtypeStruct((n_col, 2, 4 * PIECE, outs_n), bf),
+            jax.ShapeDtypeStruct((n_col, 4 * PIECE, chans), bf),
+            jax.ShapeDtypeStruct((per_z, 2, half, 128), f32),
+        ),
+        in_specs=[vm] * 3,
+        out_specs=(vm,) * 3,
+        scratch_shapes=[
+            pltpu.VMEM((3, n_col, 2, 4 * PIECE, outs_n), bf),
+            pltpu.VMEM((3, n_col, 4 * PIECE, chans), bf),
+            pltpu.VMEM((2, 6, qs + 4, SLOT, outs_n), bf),
+            pltpu.VMEM((6, qs + 4, SLOT, chans), bf),
+            pltpu.VMEM((2, n_col, nz, held, per_col, 128), bf),
+            pltpu.VMEM((18, outs_n, chans), bf),
+            pltpu.VMEM((UNITS, n_col, 2, half, 128), f32),
+            pltpu.VMEM((UNITS, n_col, half, 128), f32),
+            pltpu.VMEM((n_col, UNITS, half, 128), f32),
+            pltpu.VMEM((n_col, UNITS, half, 128), f32),
+            pltpu.VMEM((UNITS, half, 128), f32),
+            pltpu.VMEM((nz, per_z, half, 128), f32),
+            pltpu.VMEM((per_z, half, 128), f32),
+            pltpu.VMEM((per_z, half, 128), f32),
+            pltpu.VMEM((pix, outs_n), f32),
+            pltpu.VMEM((pix, chans), f32),
+            pltpu.VMEM((n_col, 2, 4 * PIECE, outs_n), bf),
+            pltpu.VMEM((n_col, 4 * PIECE, chans), bf),
+            dma((2, n_col)), dma((2, n_col)),
+            dma((2, 2, n_col)), dma((2, 2, n_col)),
+            dma((3, max(n_col, nz))), dma((3, max(n_col, nz))),
+            dma((2, n_col)), dma((2, n_col)),
+            dma((5, max(n_col, nz))), dma((5, max(n_col, nz))),
+        ],
+        compiler_params=pltpu.CompilerParams(
+            collective_id=0, has_side_effects=True, vmem_limit_bytes=48 * 1024 * 1024),
+    )(gs, xs, ks)
+    maps = om.reshape(n_col, 2, 2, 2, 12, kk, outs_n).transpose(1, 2, 4, 3, 0, 5, 6)
+    maps = maps.reshape(2, 24, 24, outs_n)
+    grad_in = oi.reshape(n_col, 2, 2, 12, kk, chans).transpose(1, 3, 2, 0, 4, 5)
+    grad_in = grad_in.reshape(24, 24, chans)
+    kg = ok.reshape(per_z, per_col, 128).transpose(1, 0, 2).reshape(per_col, per_z * 128)
+    kg = jnp.where(c == 0, kg[:, : kernels.shape[0]], kg[:, per_z * 128 - kernels.shape[0] :])
+    return maps, grad_in, kg.T
 
 
 def with_halo(x, sides, width):
@@ -72,9 +444,13 @@
 
 
 def solution(mesh):
+    n_row, n_col = mesh.shape["row"], mesh.shape["col"]
+    fits = n_col == 4 and n_row == 8
+    run = functools.partial(phased, n_row, n_col) if fits else local
+
     placed = (P("row", "col", None), P("row", "col"), P(None, "row", "col", None))
     return jax.shard_map(
-        local,
+        run,
         mesh=mesh,
         in_specs=placed,
         out_specs=(P(None, "row", "col", None), P("row", "col", None), P("row", "col")),

time: 171 us -> 53.1 us (0.31)
  Pallas kernels: 0 us -> 45 us
  waiting for transfers between devices: 43.4 us -> 0 us
  blocking collectives: 37.4 us -> 0 us
  matrix products: 30.7 us -> 0 us
  starting transfers between devices: 23.7 us -> 0 us
  between operations: 14.5 us -> 0.74 us
  other arithmetic: 8.92 us -> 1.67 us
  local copies, waits for them, and re-layouts: 11.2 us -> 5.46 us
    pallas_call x0 -> x1, Pallas kernels: none -> 45 us  [phased(): pl.pallas_call(functools.partial(kernel, n_row, n_col, scale), out_shape=...]
    all_gather x1 -> x0, blocking collectives: 37.4 us -> none  [local(): w_cols = lax.all_gather(kernels, 'col', axis=1, tiled=True)]
    dot_general x54 -> x0, matrix products: 30.7 us -> none  [the longest x18 17.4 us: local(): lax.dot_general(x_tap, g_flat, (((0,), (0,)), ((), ())), preferred_elemen...]
    ppermute x8 -> x0, starting transfers between devices: 23.6 us -> none  [the longest x4 18.3 us: with_halo(): before = lax.ppermute(last, axis, up)]
    unnamed x4 -> x0, waiting for transfers between devices: 22.4 us -> none
    ppermute x8 -> x0, waiting for transfers between devices: 17.6 us -> none  [the longest x4 17.6 us: with_halo(): after = lax.ppermute(initial, axis, down)]
    slice x2 -> x0, other arithmetic: 5.28 us -> none  [the longest x1 2.9 us: local(): g_ext[branch_index, padding_margin - shift_down:padding_margin - shift_do...]
    unnamed x102 -> x8, local copies, waits for them, and re-layouts: 8.93 us -> 4.21 us
  transfers between devices with their start and end apart: 11 -> 0, of which waited for: 3 -> 0; matrix products, arithmetic and copies ran while one was open for 26% -> 0% of each run, Pallas kernels for 0% -> 0%
where the time goes in v1:
time: 53.1 us; the launch traced here: 52.8 us
  Pallas kernels  45 us (85%)
  local copies, waits for them, and re-layouts  5.46 us (10%)
  other arithmetic  1.67 us (3%)
  between operations  0.74 us (1%)
    pallas_call x1, Pallas kernels, phased(): pl.pallas_call(functools.partial(kernel, n_row, n_col, scale), out_shape=...  45 us
    unnamed x8, local copies, waits for them, and re-layouts  4.21 us

profile of v1, /device:TPU:0, one launch (start us, length us, event | category | flops | bytes accessed | tf_op | source)
XLA Modules:
  0.0 52.8 jit_solution(8986239536308636221)
XLA Ops:
  0.6 0.9 %bitcast_bitcast_fusion.ks_ref = bf16[5,32,128]{2,1,0:T(8,128)(2,1)S(1)} fusion(bf16[32,576]{1,0:T(8,128)(2,1)} %bitcast.41, pred[]{:T(512)S(6)} %eq.6), kind=kLoop, calls=%fused_computation.3 | loop fusion | flops 20480 | bytes 77825 | tf_op jit(solution)/shard_map/transpose | solution.py:328
  1.6 1.0 %copy.13 = bf16[24,24,256]{2,0,1:T(8,128)(2,1)S(1)} copy(bf16[24,24,256]{2,1,0:T(8,128)(2,1)} %param.3) | data formatting | bytes 589824 | tf_op args[0]
  2.6 0.1 reshape.41
  2.7 0.2 copy.14
  2.9 0.0 copy-start
  3.0 0.9 %copy-done = bf16[2,24,24,128]{3,2,1,0:T(8,128)(2,1)S(1)} copy-done((bf16[2,24,24,128]{3,2,1,0:T(8,128)(2,1)S(1)}, bf16[2,24,24,128]{3,2,1,0:T(8,128)(2,1)}, u32[]{:S(2)}) %copy-start) | copy-done | bytes 294936
  3.9 0.3 copy.11
  4.2 0.2 copy.12
  4.5 45.0 %shard_map.58 = (bf16[4,2,144,128]{3,2,1,0:T(8,128)(2,1)S(1)}, bf16[4,144,256]{2,1,0:T(8,128)(2,1)S(1)}, f32[9,2,16,128]{3,2,1,0:T(8,128)S(1)}) custom-call(bf16[4,2,144,128]{3,2,1,0:T(8,128)(2,1)S(1)} %copy.16.gs_ref, bf16[4,144,256]{2,1,0:T(8,128)(2,1)S(1)} %copy.17.xs_ref, bf16[5,32,128]{2,1,0:T(8,128)(2,1)S(1)} %bitcast_bitcast_fusion.ks_ref), custom_call_target="tpu_custom_call" | custom-call | tf_op jit(solution)/shard_map/pallas_call | solution.py:336
  49.4 0.2 copy.18
  49.7 0.2 copy.19
  49.9 0.8 %copy.23 = bf16[2,24,24,128]{3,2,1,0:T(8,128)(2,1)} copy(bf16[2,24,24,128]{3,0,2,1:T(2,128)(2,1)S(1)} %bitcast.35) | data formatting | bytes 589824
  50.6 0.1 copy.22
  50.7 0.1 copy.31
  50.8 0.7 %fusion = f32[576,32]{0,1:T(8,128)} fusion(f32[32,1152]{1,0:T(8,128)S(1)} %bitcast.40, pred[]{:T(512)S(6)} %eq.6), kind=kLoop, calls=%fused_computation.2 | loop fusion | flops 18432 | bytes 221185 | tf_op jit(solution)/shard_map/transpose | solution.py:379
  51.5 0.2 copy.20
  51.7 0.2 copy.25
  51.9 1.0 %reshape.50 = bf16[24,24,256]{2,1,0:T(8,128)(2,1)} reshape(bf16[2,12,2,4,3,256]{5,4,3,2,1,0:T(4,128)(2,1)S(1)} %copy.25) | data formatting | bytes 589824
  (2 shorter events, 0.1 us)
Async XLA Ops:
  2.9 1.0 %copy-start = (bf16[2,24,24,128]{3,2,1,0:T(8,128)(2,1)S(1)}, bf16[2,24,24,128]{3,2,1,0:T(8,128)(2,1)}, u32[]{:S(2)}) copy-start(bf16[2,24,24,128]{3,2,1,0:T(8,128)(2,1)} %param.5) | copy-start | bytes 884740

commit v2 on v1

v2 whole, which is shorter than its diff:
```python
import functools

import jax
import jax.numpy as jnp
from jax import lax
from jax.experimental import pallas as pl
from jax.experimental.pallas import tpu as pltpu
from jax.sharding import PartitionSpec as P

FIRST_SPACING = 12
SECOND_SPACING = 24
UNITS = 36
SLOT = 48
MESH = pl.DeviceIdType.MESH


def kernel(n_row, n_col, scale, gs_ref, xs_ref, ks_ref, om_ref, oi_ref, ok_ref,
           ga, xa, gp, xp, kb, k2, ru, ra, sb, rb1, rb2, tc, rc, fin, fx, macc, iacc, ms, igs,
           a_send, a_recv, h_send, h_recv, k_send, k_recv, o_send, o_recv,
           p_send, p_recv, s_send, s_recv, q_send, q_recv, z_send, z_recv, l_send, l_recv):
    nz = n_row // 2
    per_z = UNITS // nz
    r = lax.axis_index("row")
    j = lax.axis_index("col")
    z = r // 2
    c = r % 2
    sib = r + 1 - 2 * c
    cols = [lax.rem(j + i, n_col) for i in range(1, n_col)]
    zs = [lax.rem(z + i, nz) for i in range(1, nz)]
    across = j + 1 - 2 * (j % 2)
    along = j + 2 - 4 * (j // 2)
    first = jnp.where(c == 0, across, along)
    second = jnp.where(c == 0, along, across)
    corner = first + second - j
    far = r - 1 + 2 * c
    has_up = r > 0
    has_down = r < n_row - 1
    has_far = jnp.where(c == 0, has_up, has_down)

    barrier = pltpu.get_barrier_semaphore()
    for s in cols:
        pl.semaphore_signal(barrier, inc=1, device_id={"col": s}, device_id_type=MESH)
    for zz in zs:
        pl.semaphore_signal(barrier, inc=1, device_id={"row": zz * 2 + c}, device_id_type=MESH)
    pl.semaphore_signal(barrier, inc=1, device_id={"row": sib}, device_id_type=MESH)

    @pl.when(has_far)
    def _():
        pl.semaphore_signal(barrier, inc=1, device_id={"row": far}, device_id_type=MESH)

    pl.semaphore_wait(barrier, n_col - 1 + nz - 1 + 1 + jnp.where(has_far, 1, 0))

    def remote(src, dst, ssem, rsem, dev):
        return pltpu.make_async_remote_copy(
            src_ref=src, dst_ref=dst, send_sem=ssem, recv_sem=rsem,
            device_id=dev, device_id_type=MESH)

    def deal(a, s):
        if a == 0:
            src, dst = gs_ref.at[:, :, s], ga.at[1, j]
        else:
            src, dst = xs_ref.at[:, s], xa.at[1, j]
        return remote(src, dst, a_send.at[a, s], a_recv.at[a, j], {"col": s})

    def dealt(a, s):
        if a == 0:
            src, dst = gs_ref.at[:, :, s], ga.at[1, s]
        else:
            src, dst = xs_ref.at[:, s], xa.at[1, s]
        return remote(src, dst, a_send.at[a, s], a_recv.at[a, s], {"col": s})

    sends = []

    def go(cp):
        cp.start()
        sends.append(cp)

    for s in cols:
        go(deal(0, s))
    for zz in zs:
        go(remote(ks_ref, kb.at[c, j, z], k_send.at[0, zz], k_recv.at[0, z], {"row": zz * 2 + c}))
    for s in cols:
        go(deal(1, s))
    kb[c, j, z] = ks_ref[...]
    ga[1, j] = gs_ref[:, :, j]
    xa[1, j] = xs_ref[:, j]

    def halo(a, s, up):
        buf = ga if a == 0 else xa
        to = r - 1 if up else r + 1
        d = 0 if up else 1
        return remote(buf.at[1, s], buf.at[2 if up else 0, s],
                      h_send.at[a, d, s], h_recv.at[a, d, s], {"row": to})

    def spread(a, s):
        @pl.when(has_up)
        def _():
            halo(a, s, True).start()

        @pl.when(has_down)
        def _():
            halo(a, s, False).start()

    def gather(a):
        for i in range(1, n_col):
            s = lax.rem(j + n_col - i, n_col)
            dealt(a, s).wait_recv()
            spread(a, s)

    def halo_wait(a):
        for s in range(n_col):
            @pl.when(has_down)
            def _():
                halo(a, s, True).wait_recv()

            @pl.when(has_up)
            def _():
                halo(a, s, False).wait_recv()

    def halo_done(a):
        for s in range(n_col):
            @pl.when(has_up)
            def _():
                halo(a, s, True).wait_send()

            @pl.when(has_down)
            def _():
                halo(a, s, False).wait_send()

    spread(0, j)
    gp[...] = jnp.zeros_like(gp)
    xp[...] = jnp.zeros_like(xp)
    gather(0)
    for i in range(1, nz):
        zz = lax.rem(z + nz - i, nz)
        remote(ks_ref, kb.at[c, j, zz], k_send.at[0, zz], k_recv.at[0, zz], {"row": zz * 2 + c}).wait_recv()

    def share(n, s, to):
        return remote(kb.at[c, s], kb.at[c, s], k_send.at[1, n], k_recv.at[1, n], {"col": to})

    go(share(0, j, first))
    go(share(1, j, second))
    spread(1, j)
    gather(1)

    def place(n):
        for s in range(n_col):
            for b in range(2):
                block = ga[n, s, b].astype(jnp.float32)
                for h in range(2):
                    part = block[:, :, 12 * h : 12 * (h + 1)].astype(jnp.bfloat16)
                    gp[b, 2 * n : 2 * n + 2, 2 + 2 * s + h, :, 0:12, :] = part

    def place_x(n):
        for s in range(n_col):
            block = xa[n, s].astype(jnp.float32)
            for h in range(2):
                part = block[:, :, 12 * h : 12 * (h + 1)].astype(jnp.bfloat16)
                xp[2 * n : 2 * n + 2, 2 + 2 * s + h, :, 0:12, :] = part

    place(1)
    place_x(1)
    share(0, first, first).wait_recv()
    go(share(2, first, second))
    halo_wait(0)

    @pl.when(has_up)
    def _():
        place(0)

    @pl.when(has_down)
    def _():
        place(2)

    qs = 2 * n_col
    outs_n = gp.shape[-1]
    chans = xp.shape[-1]
    pix = 2 * qs * SLOT
    half = outs_n // n_col // 2

    def g_tap(b, t):
        d = 1 + b
        sy = (t // 3 - 1) * d
        sx = (t % 3 - 1) * d
        return gp[b, pl.ds(2 - sy, 2), pl.ds(2 - sx, qs)].reshape(pix, outs_n)

    def x_tap(b, t):
        d = 1 + b
        sy = (t // 3 - 1) * d
        sx = (t % 3 - 1) * d
        return xp[pl.ds(2 + sy, 2), pl.ds(2 + sx, qs)].reshape(pix, chans)

    def pair(b):
        us = pl.ds(18 * b, 18)
        return remote(ru.at[us, :, 1 - c], ra.at[us], p_send.at[b], p_recv.at[b], {"row": sib})

    def step(b, k):
        us = pl.ds(18 * b, 18)
        return remote(sb.at[first if k == 0 else corner, us], rb1.at[k, us],
                      s_send.at[b, k], s_recv.at[b, k], {"col": first})

    def close(b):
        us = pl.ds(18 * b, 18)
        return remote(sb.at[second, us], rb2.at[us], q_send.at[b], q_recv.at[b], {"col": second})

    def spine(zz, at):
        return remote(tc.at[pl.ds(zz * per_z, per_z)], rc.at[at], z_send.at[zz], z_recv.at[at],
                      {"row": zz * 2 + c})

    for b in (1, 0):
        def body(t, carry):
            x_here = xp[pl.ds(2, 2), pl.ds(2, qs)].reshape(pix, chans)
            res = lax.dot_general(g_tap(b, t), x_here, (((0,), (0,)), ((), ())),
                                  preferred_element_type=jnp.float32)
            for h in range(2):
                ru[2 * (9 * b + t) + h] = res[:, 128 * h : 128 * (h + 1)].reshape(n_col, 2, half, 128)
            return carry

        lax.fori_loop(0, 9, body, 0)
        pair(b).start()

    for b in (1, 0):
        us = pl.ds(18 * b, 18)
        pair(b).wait_recv()
        for s in range(n_col):
            sb[s, us] = ru[us, s, c] + ra[us, s]
        for k in (1, 0):
            step(b, k).start()

    share(1, second, second).wait_recv()
    share(2, corner, second).wait_recv()
    swap = remote(kb.at[c], kb.at[c], k_send.at[2, 0], k_recv.at[2, 0], {"row": sib})
    go(swap)

    def reduce_plane(b):
        us = pl.ds(18 * b, 18)
        step(b, 1).wait_recv()
        sb[second, us] = sb[second, us] + rb1[1, us]
        close(b).start()
        step(b, 0).wait_recv()
        sb[j, us] = sb[j, us] + rb1[0, us]

    def reduce_spine(b):
        us = pl.ds(18 * b, 18)
        close(b).wait_recv()
        tc[us] = sb[j, us] + rb2[us]
        for zz in zs:
            @pl.when(zz // (nz // 2) == b)
            def _():
                spine(zz, z).start()

    reduce_plane(1)
    remote(kb.at[1 - c], kb.at[1 - c], k_send.at[2, 0], k_recv.at[2, 0], {"row": sib}).wait_recv()
    for u in range(UNITS):
        zz, v = divmod(u, per_z)
        mid = per_z // 2
        if v < mid:
            val = kb[0, :, zz, v]
        elif v > mid:
            val = kb[1, :, zz, v - mid]
        else:
            val = kb[0, :, zz, mid] + kb[1, :, zz, 0]
        k2[u // 2, :, 128 * (u % 2) : 128 * (u % 2 + 1)] = val.reshape(outs_n, 128)

    def pack(acc, s):
        halves = [acc[:, 2 * s + h, :, 0:12, :] for h in range(2)]
        return jnp.concatenate(halves, axis=2).astype(jnp.bfloat16)

    def back(k, s, at):
        if k == 2:
            src, dst = igs.at[s], oi_ref.at[:, at]
        else:
            src, dst = ms.at[s, k], om_ref.at[k, :, at]
        return remote(src, dst, o_send.at[k, s], o_recv.at[k, at], {"col": s})

    def input_part(b):
        def body(t, carry):
            res = jnp.dot(g_tap(b, t), k2[9 * b + t], preferred_element_type=jnp.float32)
            iacc[...] += res.reshape(iacc.shape)
            return carry

        lax.fori_loop(0, 9, body, 0)

    def map_part(b):
        macc[...] = jnp.zeros_like(macc)

        def body(t, carry):
            res = lax.dot_general(x_tap(b, t), k2[9 * b + t], (((1,), (1,)), ((), ())),
                                  preferred_element_type=jnp.float32)
            macc[...] += res.reshape(macc.shape)
            return carry

        lax.fori_loop(0, 9, body, 0)
        for s in range(n_col):
            ms[s, b] = pack(macc, s)
        for s in cols:
            back(b, s, j).start()
        om_ref[b, :, j] = ms[j, b]

    iacc[...] = jnp.zeros_like(iacc)
    input_part(0)
    reduce_plane(0)
    input_part(1)
    for s in range(n_col):
        igs[s] = pack(iacc, s)
    for s in cols:
        back(2, s, j).start()
    oi_ref[:, j] = igs[j]
    reduce_spine(1)

    halo_wait(1)

    @pl.when(has_up)
    def _():
        place_x(0)

    @pl.when(has_down)
    def _():
        place_x(2)

    map_part(0)
    reduce_spine(0)
    map_part(1)

    mine = tc[pl.ds(z * per_z, per_z)]
    for i in range(1, nz):
        zz = lax.rem(z + nz - i, nz)
        spine(zz, zz).wait_recv()
        mine = mine + rc[zz]
    fin[...] = mine * scale
    last = remote(fin, fx, l_send.at[0], l_recv.at[0], {"row": sib})
    last.start()
    ok_ref[:, c] = fin[...]
    last.wait()
    ok_ref[:, 1 - c] = fx[...]

    for k in range(3):
        for i in range(1, n_col):
            s = lax.rem(j + n_col - i, n_col)
            back(k, s, s).wait_recv()
        for s in cols:
            back(k, s, j).wait_send()
    for b in (1, 0):
        pair(b).wait_send()
        for k in (1, 0):
            step(b, k).wait_send()
        close(b).wait_send()
    for zz in zs:
        spine(zz, z).wait_send()
    for cp in sends:
        cp.wait_send()
    halo_done(0)
    halo_done(1)


def phased(n_row, n_col, features, kernels, out_cotangent):
    nz = n_row // 2
    per_z = UNITS // nz
    rows_dev, cols_dev, chans = features.shape
    outs_n = out_cotangent.shape[3]
    kk = 12 // n_col
    per_col = outs_n // n_col
    c = lax.axis_index("row") % 2
    bf, f32 = jnp.bfloat16, jnp.float32
    xs = features.reshape(2, n_col, kk, cols_dev, chans)
    gs = out_cotangent.reshape(2, 2, n_col, kk, cols_dev, outs_n)
    kt = kernels.T
    kt = jnp.where(c == 0, jnp.pad(kt, ((0, 0), (0, 64))), jnp.pad(kt, ((0, 0), (64, 0))))
    held = (per_z + 1) // 2
    ks = kt.reshape(per_col, held, 128).transpose(1, 0, 2)
    cells = rows_dev * n_row * cols_dev * n_col
    scale = 1.0 / float(cells) ** 0.5
    qs = 2 * n_col
    half = per_col // 2
    vm = pl.BlockSpec(memory_space=pltpu.VMEM)
    dma = pltpu.SemaphoreType.DMA
    om, oi, ok = pl.pallas_call(
        functools.partial(kernel, n_row, n_col, scale),
        out_shape=(
            jax.ShapeDtypeStruct(gs.shape, bf),
            jax.ShapeDtypeStruct(xs.shape, bf),
            jax.ShapeDtypeStruct((per_z, 2, half, 128), f32),
        ),
        in_specs=[vm] * 3,
        out_specs=(vm,) * 3,
        scratch_shapes=[
            pltpu.VMEM((3, n_col, 2, 2, kk, cols_dev, outs_n), bf),
            pltpu.VMEM((3, n_col, 2, kk, cols_dev, chans), bf),
            pltpu.VMEM((2, 6, qs + 4, kk, 16, outs_n), bf),
            pltpu.VMEM((6, qs + 4, kk, 16, chans), bf),
            pltpu.VMEM((2, n_col, nz, held, per_col, 128), bf),
            pltpu.VMEM((18, outs_n, chans), bf),
            pltpu.VMEM((UNITS, n_col, 2, half, 128), f32),
            pltpu.VMEM((UNITS, n_col, half, 128), f32),
            pltpu.VMEM((n_col, UNITS, half, 128), f32),
            pltpu.VMEM((2, UNITS, half, 128), f32),
            pltpu.VMEM((UNITS, half, 128), f32),
            pltpu.VMEM((UNITS, half, 128), f32),
            pltpu.VMEM((nz, per_z, half, 128), f32),
            pltpu.VMEM((per_z, half, 128), f32),
            pltpu.VMEM((per_z, half, 128), f32),
            pltpu.VMEM((2, qs, kk, 16, outs_n), f32),
            pltpu.VMEM((2, qs, kk, 16, chans), f32),
            pltpu.VMEM((n_col, 2, 2, kk, cols_dev, outs_n), bf),
            pltpu.VMEM((n_col, 2, kk, cols_dev, chans), bf),
            dma((2, n_col)), dma((2, n_col)),
            dma((2, 2, n_col)), dma((2, 2, n_col)),
            dma((3, 4)), dma((3, 4)),
            dma((3, n_col)), dma((3, n_col)),
            dma((2,)), dma((2,)),
            dma((2, 2)), dma((2, 2)),
            dma((2,)), dma((2,)),
            dma((nz,)), dma((nz,)),
            dma((1,)), dma((1,)),
        ],
        compiler_params=pltpu.CompilerParams(
            collective_id=0, has_side_effects=True, vmem_limit_bytes=48 * 1024 * 1024),
    )(gs, xs, ks)
    kg = ok.reshape(per_z, per_col, 128).transpose(1, 0, 2).reshape(per_col, per_z * 128)
    kg = jnp.where(c == 0, kg[:, : kernels.shape[0]], kg[:, per_z * 128 - kernels.shape[0] :])
    return om.reshape(out_cotangent.shape), oi.reshape(features.shape), kg.T


def with_halo(x, sides, width):
    for axis, dim in sides:
        size, length = (lax.axis_size(axis), x.shape[dim])
        up = [(i, (i + 1) % size) for i in range(size - 1)]
        down = [(j, i) for i, j in up]
        last = lax.slice_in_dim(x, length - width, length, axis=dim)
        initial = lax.slice_in_dim(x, 0, width, axis=dim)
        before = lax.ppermute(last, axis, up)
        after = lax.ppermute(initial, axis, down)
        x = jnp.concatenate([before, x, after], axis=dim)
    return x


def local(features, kernels, out_cotangent):
    rows_dev = features.shape[0]
    cols_dev = features.shape[1]
    chans = features.shape[2]
    outs_n = out_cotangent.shape[3]
    padding_margin = SECOND_SPACING
    x_ext = with_halo(features, (("row", 0), ("col", 1)), padding_margin)
    g_ext = with_halo(out_cotangent, (("row", 1), ("col", 2)), padding_margin)
    w_cols = lax.all_gather(kernels, "col", axis=1, tiled=True)
    w_full = lax.all_gather(w_cols, "row", axis=0, tiled=True)
    w_blocks = w_full.reshape(2, 9, chans, outs_n)
    pixels = rows_dev * cols_dev
    maps = []
    grads = []
    grad_in = jnp.zeros((pixels, chans), jnp.float32)
    for branch_index, dilation_rate in ((0, FIRST_SPACING), (1, SECOND_SPACING)):
        result = jnp.zeros((pixels, outs_n), jnp.float32)
        g_flat = out_cotangent[branch_index].reshape(pixels, outs_n)
        for kernel_tap in range(9):
            shift_down = (kernel_tap // 3 - 1) * dilation_rate
            shift_across = (kernel_tap % 3 - 1) * dilation_rate
            x_tap = x_ext[
                padding_margin + shift_down : padding_margin + shift_down + rows_dev,
                padding_margin + shift_across : padding_margin + shift_across + cols_dev,
            ].reshape(pixels, chans)
            g_tap = g_ext[
                branch_index,
                padding_margin - shift_down : padding_margin - shift_down + rows_dev,
                padding_margin - shift_across : padding_margin - shift_across + cols_dev,
            ].reshape(pixels, outs_n)
            weight = w_blocks[branch_index, kernel_tap]
            result = result + jnp.dot(x_tap, weight, preferred_element_type=jnp.float32)
            grad_in = grad_in + lax.dot_general(
                g_tap, weight, (((1,), (1,)), ((), ())), preferred_element_type=jnp.float32
            )
            grads.append(
                lax.dot_general(
                    x_tap, g_flat, (((0,), (0,)), ((), ())), preferred_element_type=jnp.float32
                )
            )
        maps.append(result.reshape(rows_dev, cols_dev, outs_n).astype(jnp.bfloat16))
    branch_maps = jnp.stack(maps, 0)
    input_grad = grad_in.reshape(rows_dev, cols_dev, chans).astype(jnp.bfloat16)
    local_grad = jnp.concatenate(grads, 0)
    total_cells = rows_dev * lax.axis_size("row") * cols_dev * lax.axis_size("col")
    scale = 1.0 / jnp.sqrt(jnp.float32(total_cells))
    partial_grad = lax.psum_scatter(local_grad, "row", scatter_dimension=0, tiled=True)
    kernel_grad = lax.psum_scatter(partial_grad, "col", scatter_dimension=1, tiled=True)
    return (branch_maps, input_grad, kernel_grad * scale)


def solution(mesh):
    n_row, n_col = mesh.shape["row"], mesh.shape["col"]
    fits = n_col == 4 and n_row == 8
    run = functools.partial(phased, n_row, n_col) if fits else local

    placed = (P("row", "col", None), P("row", "col"), P(None, "row", "col", None))
    return jax.shard_map(
        run,
        mesh=mesh,
        in_specs=placed,
        out_specs=(P(None, "row", "col", None), P("row", "col", None), P("row", "col")),
        check_vma=False,
    )
```

time: 53.1 us -> 52.2 us (0.983)
  local copies, waits for them, and re-layouts: 5.46 us -> 3.49 us
  Pallas kernels: 45 us -> 46.1 us
    pallas_call x1, Pallas kernels: 45 us -> 46.1 us  [phased(): pl.pallas_call(functools.partial(kernel, n_row, n_col, scale), out_shape=...]
    unnamed x8 -> x7, local copies, waits for them, and re-layouts: 4.21 us -> 3.4 us
    transpose x3 -> x0, local copies, waits for them, and re-layouts: 0.64 us -> none  [the longest x1 0.23 us: phased(): features.reshape(2, 12, 2, n_col, kk, chans).transpose(3, 0, 2, 1, 4, 5)]
where the time goes in v2:
time: 52.2 us; the launch traced here: 51.9 us
  Pallas kernels  46.1 us (88%)
  local copies, waits for them, and re-layouts  3.49 us (7%)
  other arithmetic  1.67 us (3%)
  between operations  0.68 us (1%)
    pallas_call x1, Pallas kernels, phased(): pl.pallas_call(functools.partial(kernel, n_row, n_col, scale), out_shape=...  46.1 us
    unnamed x7, local copies, waits for them, and re-layouts  3.4 us

profile of v2, /device:TPU:0, one launch (start us, length us, event | category | flops | bytes accessed | tf_op | source)
XLA Modules:
  0.0 51.9 jit_solution(7597096113901335320)
XLA Ops:
  0.6 0.9 %bitcast_bitcast_fusion.ks_ref = bf16[5,32,128]{2,1,0:T(8,128)(2,1)S(1)} fusion(bf16[32,576]{1,0:T(8,128)(2,1)} %bitcast.27, pred[]{:T(512)S(6)} %eq.6), kind=kLoop, calls=%fused_computation.3 | loop fusion | flops 20480 | bytes 77825 | tf_op jit(solution)/shard_map/transpose | solution.py:370
  1.6 0.0 copy-start
  1.6 1.0 %copy-done = bf16[2,24,24,128]{3,2,1,0:T(8,128)(2,1)S(1)} copy-done((bf16[2,24,24,128]{3,2,1,0:T(8,128)(2,1)S(1)}, bf16[2,24,24,128]{3,2,1,0:T(8,128)(2,1)}, u32[]{:S(2)}) %copy-start) | copy-done | bytes 294936
  2.6 0.0 copy-start.1
  2.6 1.0 %copy-done.1 = bf16[24,24,256]{2,1,0:T(8,128)(2,1)S(1)} copy-done((bf16[24,24,256]{2,1,0:T(8,128)(2,1)S(1)}, bf16[24,24,256]{2,1,0:T(8,128)(2,1)}, u32[]{:S(2)}) %copy-start.1) | copy-done | bytes 294936
  3.5 46.1 %shard_map.58 = (bf16[2,2,4,3,24,128]{5,4,3,2,1,0:T(8,128)(2,1)S(1)}, bf16[2,4,3,24,256]{4,3,2,1,0:T(8,128)(2,1)S(1)}, f32[9,2,16,128]{3,2,1,0:T(8,128)S(1)}) custom-call(bf16[2,2,4,3,24,128]{5,4,3,2,1,0:T(8,128)(2,1)S(1)} %bitcast.20, bf16[2,4,3,24,256]{4,3,2,1,0:T(8,128)(2,1)S(1)} %bitcast.21, bf16[5,32,128]{2,1,0:T(8,128)(2,1)S(1)} %bitcast_bitcast_fusion.ks_ref), custom_call_target="tpu_custom_call" | custom-call | tf_op jit(solution)/shard_map/pallas_call | solution.py:377
  49.6 0.1 copy.8
  49.7 0.1 copy.13
  49.8 0.7 %fusion = f32[576,32]{0,1:T(8,128)} fusion(f32[32,1152]{1,0:T(8,128)S(1)} %bitcast.26, pred[]{:T(512)S(6)} %eq.6), kind=kLoop, calls=%fused_computation.2 | loop fusion | flops 18432 | bytes 221185 | tf_op jit(solution)/shard_map/transpose | solution.py:421
  50.5 0.7 %copy.16 = bf16[2,24,24,128]{3,2,1,0:T(8,128)(2,1)} copy(bf16[2,24,24,128]{3,2,1,0:T(8,128)(2,1)S(1)} %bitcast.23) | data formatting | bytes 589824
  51.2 0.7 %copy.17 = bf16[24,24,256]{2,1,0:T(8,128)(2,1)} copy(bf16[24,24,256]{2,1,0:T(8,128)(2,1)S(1)} %bitcast.22) | data formatting | bytes 589824
Async XLA Ops:
  1.6 1.0 %copy-start = (bf16[2,24,24,128]{3,2,1,0:T(8,128)(2,1)S(1)}, bf16[2,24,24,128]{3,2,1,0:T(8,128)(2,1)}, u32[]{:S(2)}) copy-start(bf16[2,24,24,128]{3,2,1,0:T(8,128)(2,1)} %param.5) | copy-start | bytes 884740
  2.6 1.0 %copy-start.1 = (bf16[24,24,256]{2,1,0:T(8,128)(2,1)S(1)}, bf16[24,24,256]{2,1,0:T(8,128)(2,1)}, u32[]{:S(2)}) copy-start(bf16[24,24,256]{2,1,0:T(8,128)(2,1)} %param.3) | copy-start | bytes 884740

commit v3 on v2

--- a/solution.py
+++ b/solution.py
@@ -17,7 +17,7 @@
 def kernel(n_row, n_col, scale, gs_ref, xs_ref, ks_ref, om_ref, oi_ref, ok_ref,
            ga, xa, gp, xp, kb, k2, ru, ra, sb, rb1, rb2, tc, rc, fin, fx, macc, iacc, ms, igs,
            a_send, a_recv, h_send, h_recv, k_send, k_recv, o_send, o_recv,
-           p_send, p_recv, s_send, s_recv, q_send, q_recv, z_send, z_recv, l_send, l_recv):
+           p_send, p_recv, s_send, s_recv, q_send, q_recv, z_send, z_recv, l_send, l_recv, own_sem):
     nz = n_row // 2
     per_z = UNITS // nz
     r = lax.axis_index("row")
@@ -82,8 +82,10 @@
     for s in cols:
         go(deal(1, s))
     kb[c, j, z] = ks_ref[...]
-    ga[1, j] = gs_ref[:, :, j]
-    xa[1, j] = xs_ref[:, j]
+    own_g = pltpu.make_async_copy(gs_ref.at[:, :, j], ga.at[1, j], own_sem.at[0])
+    own_x = pltpu.make_async_copy(xs_ref.at[:, j], xa.at[1, j], own_sem.at[1])
+    own_g.start()
+    own_x.start()
 
     def halo(a, s, up):
         buf = ga if a == 0 else xa
@@ -127,9 +129,10 @@
             def _():
                 halo(a, s, False).wait_send()
 
-    spread(0, j)
     gp[...] = jnp.zeros_like(gp)
     xp[...] = jnp.zeros_like(xp)
+    own_g.wait()
+    spread(0, j)
     gather(0)
     for i in range(1, nz):
         zz = lax.rem(z + nz - i, nz)
@@ -140,6 +143,7 @@
 
     go(share(0, j, first))
     go(share(1, j, second))
+    own_x.wait()
     spread(1, j)
     gather(1)
 
@@ -158,20 +162,6 @@
                 part = block[:, :, 12 * h : 12 * (h + 1)].astype(jnp.bfloat16)
                 xp[2 * n : 2 * n + 2, 2 + 2 * s + h, :, 0:12, :] = part
 
-    place(1)
-    place_x(1)
-    share(0, first, first).wait_recv()
-    go(share(2, first, second))
-    halo_wait(0)
-
-    @pl.when(has_up)
-    def _():
-        place(0)
-
-    @pl.when(has_down)
-    def _():
-        place(2)
-
     qs = 2 * n_col
     outs_n = gp.shape[-1]
     chans = xp.shape[-1]
@@ -190,25 +180,31 @@
         sx = (t % 3 - 1) * d
         return xp[pl.ds(2 + sy, 2), pl.ds(2 + sx, qs)].reshape(pix, chans)
 
-    def pair(b):
-        us = pl.ds(18 * b, 18)
-        return remote(ru.at[us, :, 1 - c], ra.at[us], p_send.at[b], p_recv.at[b], {"row": sib})
-
-    def step(b, k):
-        us = pl.ds(18 * b, 18)
+    def span(g):
+        return pl.ds(6 * g, 6)
+
+    def pair(g):
+        us = span(g)
+        return remote(ru.at[us, :, 1 - c], ra.at[us], p_send.at[g], p_recv.at[g], {"row": sib})
+
+    def step(g, k):
+        us = span(g)
         return remote(sb.at[first if k == 0 else corner, us], rb1.at[k, us],
-                      s_send.at[b, k], s_recv.at[b, k], {"col": first})
-
-    def close(b):
-        us = pl.ds(18 * b, 18)
-        return remote(sb.at[second, us], rb2.at[us], q_send.at[b], q_recv.at[b], {"col": second})
-
-    def spine(zz, at):
-        return remote(tc.at[pl.ds(zz * per_z, per_z)], rc.at[at], z_send.at[zz], z_recv.at[at],
-                      {"row": zz * 2 + c})
-
-    for b in (1, 0):
-        def body(t, carry):
+                      s_send.at[g, k], s_recv.at[g, k], {"col": first})
+
+    def close(g):
+        us = span(g)
+        return remote(sb.at[second, us], rb2.at[us], q_send.at[g], q_recv.at[g], {"col": second})
+
+    def spine(zz, k, at):
+        return remote(tc.at[pl.ds(zz * per_z + 3 * k, 3)], rc.at[at, pl.ds(3 * k, 3)],
+                      z_send.at[k, zz], z_recv.at[k, at], {"row": zz * 2 + c})
+
+    def taps_grad(g):
+        b = g // 3
+
+        def body(i, carry):
+            t = 3 * (g % 3) + i
             x_here = xp[pl.ds(2, 2), pl.ds(2, qs)].reshape(pix, chans)
             res = lax.dot_general(g_tap(b, t), x_here, (((0,), (0,)), ((), ())),
                                   preferred_element_type=jnp.float32)
@@ -216,40 +212,73 @@
                 ru[2 * (9 * b + t) + h] = res[:, 128 * h : 128 * (h + 1)].reshape(n_col, 2, half, 128)
             return carry
 
-        lax.fori_loop(0, 9, body, 0)
-        pair(b).start()
-
-    for b in (1, 0):
-        us = pl.ds(18 * b, 18)
-        pair(b).wait_recv()
+        lax.fori_loop(0, 3, body, 0)
+        pair(g).start()
+
+    def reduce_pair(g):
+        us = span(g)
+        pair(g).wait_recv()
         for s in range(n_col):
             sb[s, us] = ru[us, s, c] + ra[us, s]
         for k in (1, 0):
-            step(b, k).start()
+            step(g, k).start()
+
+    def reduce_plane(g):
+        us = span(g)
+        step(g, 1).wait_recv()
+        sb[second, us] = sb[second, us] + rb1[1, us]
+        close(g).start()
+        step(g, 0).wait_recv()
+        sb[j, us] = sb[j, us] + rb1[0, us]
+
+    def reduce_spine(g):
+        us = span(g)
+        close(g).wait_recv()
+        tc[us] = sb[j, us] + rb2[us]
+        for q in (2 * g, 2 * g + 1):
+            @pl.when(z != 3 * q // per_z)
+            def _():
+                spine(3 * q // per_z, q % (per_z // 3), z).start()
+
+    place(1)
+    place_x(1)
+    taps_grad(1)
+    share(0, first, first).wait_recv()
+    taps_grad(4)
+    reduce_pair(1)
+    halo_wait(0)
+
+    @pl.when(has_up)
+    def _():
+        place(0)
+
+    @pl.when(has_down)
+    def _():
+        place(2)
+
+    reduce_pair(4)
+    taps_grad(3)
+    go(share(2, first, second))
+    reduce_plane(1)
+    taps_grad(5)
+    reduce_pair(3)
+    reduce_plane(4)
+    taps_grad(0)
+    reduce_pair(5)
+    reduce_spine(1)
+    taps_grad(2)
+    reduce_pair(0)
+    reduce_plane(3)
+    reduce_spine(4)
+    reduce_pair(2)
+    reduce_plane(5)
 
     share(1, second, second).wait_recv()
     share(2, corner, second).wait_recv()
     swap = remote(kb.at[c], kb.at[c], k_send.at[2, 0], k_recv.at[2, 0], {"row": sib})
     go(swap)
-
-    def reduce_plane(b):
-        us = pl.ds(18 * b, 18)
-        step(b, 1).wait_recv()
-        sb[second, us] = sb[second, us] + rb1[1, us]
-        close(b).start()
-        step(b, 0).wait_recv()
-        sb[j, us] = sb[j, us] + rb1[0, us]
-
-    def reduce_spine(b):
-        us = pl.ds(18 * b, 18)
-        close(b).wait_recv()
-        tc[us] = sb[j, us] + rb2[us]
-        for zz in zs:
-            @pl.when(zz // (nz // 2) == b)
-            def _():
-                spine(zz, z).start()
-
-    reduce_plane(1)
+    reduce_spine(3)
+    reduce_plane(0)
     remote(kb.at[1 - c], kb.at[1 - c], k_send.at[2, 0], k_recv.at[2, 0], {"row": sib}).wait_recv()
     for u in range(UNITS):
         zz, v = divmod(u, per_z)
@@ -299,14 +328,16 @@
 
     iacc[...] = jnp.zeros_like(iacc)
     input_part(0)
-    reduce_plane(0)
+    reduce_plane(2)
+    reduce_spine(5)
+    reduce_spine(0)
     input_part(1)
     for s in range(n_col):
         igs[s] = pack(iacc, s)
     for s in cols:
         back(2, s, j).start()
     oi_ref[:, j] = igs[j]
-    reduce_spine(1)
+    reduce_spine(2)
 
     halo_wait(1)
 
@@ -319,18 +350,17 @@
         place_x(2)
 
     map_part(0)
-    reduce_spine(0)
-    map_part(1)
-
     mine = tc[pl.ds(z * per_z, per_z)]
     for i in range(1, nz):
         zz = lax.rem(z + nz - i, nz)
-        spine(zz, zz).wait_recv()
+        for k in range(per_z // 3):
+            spine(zz, k, zz).wait_recv()
         mine = mine + rc[zz]
     fin[...] = mine * scale
     last = remote(fin, fx, l_send.at[0], l_recv.at[0], {"row": sib})
     last.start()
     ok_ref[:, c] = fin[...]
+    map_part(1)
     last.wait()
     ok_ref[:, 1 - c] = fx[...]
 
@@ -340,13 +370,14 @@
             back(k, s, s).wait_recv()
         for s in cols:
             back(k, s, j).wait_send()
-    for b in (1, 0):
-        pair(b).wait_send()
+    for g in range(6):
+        pair(g).wait_send()
         for k in (1, 0):
-            step(b, k).wait_send()
-        close(b).wait_send()
+            step(g, k).wait_send()
+        close(g).wait_send()
     for zz in zs:
-        spine(zz, z).wait_send()
+        for k in range(per_z // 3):
+            spine(zz, k, z).wait_send()
     for cp in sends:
         cp.wait_send()
     halo_done(0)
@@ -381,7 +412,7 @@
             jax.ShapeDtypeStruct(xs.shape, bf),
             jax.ShapeDtypeStruct((per_z, 2, half, 128), f32),
         ),
-        in_specs=[vm] * 3,
+        in_specs=[pl.BlockSpec(memory_space=pltpu.HBM)] * 2 + [vm],
         out_specs=(vm,) * 3,
         scratch_shapes=[
             pltpu.VMEM((3, n_col, 2, 2, kk, cols_dev, outs_n), bf),
@@ -407,11 +438,12 @@
             dma((2, 2, n_col)), dma((2, 2, n_col)),
             dma((3, 4)), dma((3, 4)),
             dma((3, n_col)), dma((3, n_col)),
-            dma((2,)), dma((2,)),
-            dma((2, 2)), dma((2, 2)),
-            dma((2,)), dma((2,)),
-            dma((nz,)), dma((nz,)),
+            dma((6,)), dma((6,)),
+            dma((6, 2)), dma((6, 2)),
+            dma((6,)), dma((6,)),
+            dma((per_z // 3, nz)), dma((per_z // 3, nz)),
             dma((1,)), dma((1,)),
+            dma((2,)),
         ],
         compiler_params=pltpu.CompilerParams(
             collective_id=0, has_side_effects=True, vmem_limit_bytes=48 * 1024 * 1024),

time: 52.2 us -> 52.3 us (level)
  no operation moved by 1% of the time
where the time goes in v3:
time: 52.3 us; the launch traced here: 52 us
  Pallas kernels  46.2 us (88%)
  local copies, waits for them, and re-layouts  3.49 us (7%)
  other arithmetic  1.67 us (3%)
  between operations  0.68 us (1%)
    pallas_call x1, Pallas kernels, phased(): pl.pallas_call(functools.partial(kernel, n_row, n_col, scale), out_shape=...  46.2 us
    unnamed x7, local copies, waits for them, and re-layouts  3.4 us

profile of v3, /device:TPU:0, one launch (start us, length us, event | category | flops | bytes accessed | tf_op | source)
XLA Modules:
  0.0 52.0 jit_solution(6703982899506266902)
XLA Ops:
  0.6 0.9 %bitcast_bitcast_fusion.ks_ref = bf16[5,32,128]{2,1,0:T(8,128)(2,1)S(1)} fusion(bf16[32,576]{1,0:T(8,128)(2,1)} %bitcast.27, pred[]{:T(512)S(6)} %eq.6), kind=kLoop, calls=%fused_computation.3 | loop fusion | flops 20480 | bytes 77825 | tf_op jit(solution)/shard_map/transpose | solution.py:401
  1.6 0.0 copy-start
  1.6 1.0 %copy-done = bf16[2,24,24,128]{3,2,1,0:T(8,128)(2,1)S(1)} copy-done((bf16[2,24,24,128]{3,2,1,0:T(8,128)(2,1)S(1)}, bf16[2,24,24,128]{3,2,1,0:T(8,128)(2,1)}, u32[]{:S(2)}) %copy-start) | copy-done | bytes 294936
  2.6 0.0 copy-start.1
  2.6 1.0 %copy-done.1 = bf16[24,24,256]{2,1,0:T(8,128)(2,1)S(1)} copy-done((bf16[24,24,256]{2,1,0:T(8,128)(2,1)S(1)}, bf16[24,24,256]{2,1,0:T(8,128)(2,1)}, u32[]{:S(2)}) %copy-start.1) | copy-done | bytes 294936
  3.5 46.2 %shard_map.58 = (bf16[2,2,4,3,24,128]{5,4,3,2,1,0:T(8,128)(2,1)S(1)}, bf16[2,4,3,24,256]{4,3,2,1,0:T(8,128)(2,1)S(1)}, f32[9,2,16,128]{3,2,1,0:T(8,128)S(1)}) custom-call(bf16[2,2,4,3,24,128]{5,4,3,2,1,0:T(8,128)(2,1)S(1)} %bitcast.20, bf16[2,4,3,24,256]{4,3,2,1,0:T(8,128)(2,1)S(1)} %bitcast.21, bf16[5,32,128]{2,1,0:T(8,128)(2,1)S(1)} %bitcast_bitcast_fusion.ks_ref), custom_call_target="tpu_custom_call" | custom-call | tf_op jit(solution)/shard_map/pallas_call | solution.py:408
  49.7 0.1 copy.8
  49.8 0.1 copy.13
  49.8 0.7 %fusion = f32[576,32]{0,1:T(8,128)} fusion(f32[32,1152]{1,0:T(8,128)S(1)} %bitcast.26, pred[]{:T(512)S(6)} %eq.6), kind=kLoop, calls=%fused_computation.2 | loop fusion | flops 18432 | bytes 221185 | tf_op jit(solution)/shard_map/transpose | solution.py:453
  50.6 0.7 %copy.16 = bf16[2,24,24,128]{3,2,1,0:T(8,128)(2,1)} copy(bf16[2,24,24,128]{3,2,1,0:T(8,128)(2,1)S(1)} %bitcast.23) | data formatting | bytes 589824
  51.3 0.7 %copy.17 = bf16[24,24,256]{2,1,0:T(8,128)(2,1)} copy(bf16[24,24,256]{2,1,0:T(8,128)(2,1)S(1)} %bitcast.22) | data formatting | bytes 589824
Async XLA Ops:
  1.6 1.0 %copy-start = (bf16[2,24,24,128]{3,2,1,0:T(8,128)(2,1)S(1)}, bf16[2,24,24,128]{3,2,1,0:T(8,128)(2,1)}, u32[]{:S(2)}) copy-start(bf16[2,24,24,128]{3,2,1,0:T(8,128)(2,1)} %param.5) | copy-start | bytes 884740
  2.6 1.0 %copy-start.1 = (bf16[24,24,256]{2,1,0:T(8,128)(2,1)S(1)}, bf16[24,24,256]{2,1,0:T(8,128)(2,1)}, u32[]{:S(2)}) copy-start(bf16[24,24,256]{2,1,0:T(8,128)(2,1)} %param.3) | copy-start | bytes 884740

commit v4 on v3

--- a/solution.py
+++ b/solution.py
@@ -129,10 +129,10 @@
             def _():
                 halo(a, s, False).wait_send()
 
+    own_g.wait()
+    spread(0, j)
     gp[...] = jnp.zeros_like(gp)
     xp[...] = jnp.zeros_like(xp)
-    own_g.wait()
-    spread(0, j)
     gather(0)
     for i in range(1, nz):
         zz = lax.rem(z + nz - i, nz)
@@ -350,6 +350,7 @@
         place_x(2)
 
     map_part(0)
+    map_part(1)
     mine = tc[pl.ds(z * per_z, per_z)]
     for i in range(1, nz):
         zz = lax.rem(z + nz - i, nz)
@@ -360,7 +361,6 @@
     last = remote(fin, fx, l_send.at[0], l_recv.at[0], {"row": sib})
     last.start()
     ok_ref[:, c] = fin[...]
-    map_part(1)
     last.wait()
     ok_ref[:, 1 - c] = fx[...]
 

time: 52.3 us -> 52.2 us (level)
  no operation moved by 1% of the time
where the time goes in v4:
time: 52.2 us; the launch traced here: 52 us
  Pallas kernels  46.1 us (88%)
  local copies, waits for them, and re-layouts  3.49 us (7%)
  other arithmetic  1.67 us (3%)
  between operations  0.68 us (1%)
    pallas_call x1, Pallas kernels, phased(): pl.pallas_call(functools.partial(kernel, n_row, n_col, scale), out_shape=...  46.1 us
    unnamed x7, local copies, waits for them, and re-layouts  3.4 us

profile of v4, /device:TPU:0, one launch (start us, length us, event | category | flops | bytes accessed | tf_op | source)
XLA Modules:
  0.0 52.0 jit_solution(10935034940693145830)
XLA Ops:
  0.6 0.9 %bitcast_bitcast_fusion.ks_ref = bf16[5,32,128]{2,1,0:T(8,128)(2,1)S(1)} fusion(bf16[32,576]{1,0:T(8,128)(2,1)} %bitcast.27, pred[]{:T(512)S(6)} %eq.6), kind=kLoop, calls=%fused_computation.3 | loop fusion | flops 20480 | bytes 77825 | tf_op jit(solution)/shard_map/transpose | solution.py:401
  1.6 0.0 copy-start
  1.6 1.0 %copy-done = bf16[2,24,24,128]{3,2,1,0:T(8,128)(2,1)S(1)} copy-done((bf16[2,24,24,128]{3,2,1,0:T(8,128)(2,1)S(1)}, bf16[2,24,24,128]{3,2,1,0:T(8,128)(2,1)}, u32[]{:S(2)}) %copy-start) | copy-done | bytes 294936
  2.6 0.0 copy-start.1
  2.6 1.0 %copy-done.1 = bf16[24,24,256]{2,1,0:T(8,128)(2,1)S(1)} copy-done((bf16[24,24,256]{2,1,0:T(8,128)(2,1)S(1)}, bf16[24,24,256]{2,1,0:T(8,128)(2,1)}, u32[]{:S(2)}) %copy-start.1) | copy-done | bytes 294936
  3.5 46.1 %shard_map.58 = (bf16[2,2,4,3,24,128]{5,4,3,2,1,0:T(8,128)(2,1)S(1)}, bf16[2,4,3,24,256]{4,3,2,1,0:T(8,128)(2,1)S(1)}, f32[9,2,16,128]{3,2,1,0:T(8,128)S(1)}) custom-call(bf16[2,2,4,3,24,128]{5,4,3,2,1,0:T(8,128)(2,1)S(1)} %bitcast.20, bf16[2,4,3,24,256]{4,3,2,1,0:T(8,128)(2,1)S(1)} %bitcast.21, bf16[5,32,128]{2,1,0:T(8,128)(2,1)S(1)} %bitcast_bitcast_fusion.ks_ref), custom_call_target="tpu_custom_call" | custom-call | tf_op jit(solution)/shard_map/pallas_call | solution.py:408
  49.6 0.1 copy.8
  49.7 0.1 copy.13
  49.8 0.7 %fusion = f32[576,32]{0,1:T(8,128)} fusion(f32[32,1152]{1,0:T(8,128)S(1)} %bitcast.26, pred[]{:T(512)S(6)} %eq.6), kind=kLoop, calls=%fused_computation.2 | loop fusion | flops 18432 | bytes 221185 | tf_op jit(solution)/shard_map/transpose | solution.py:453
  50.5 0.7 %copy.16 = bf16[2,24,24,128]{3,2,1,0:T(8,128)(2,1)} copy(bf16[2,24,24,128]{3,2,1,0:T(8,128)(2,1)S(1)} %bitcast.23) | data formatting | bytes 589824
  51.2 0.7 %copy.17 = bf16[24,24,256]{2,1,0:T(8,128)(2,1)} copy(bf16[24,24,256]{2,1,0:T(8,128)(2,1)S(1)} %bitcast.22) | data formatting | bytes 589824
Async XLA Ops:
  1.6 1.0 %copy-start = (bf16[2,24,24,128]{3,2,1,0:T(8,128)(2,1)S(1)}, bf16[2,24,24,128]{3,2,1,0:T(8,128)(2,1)}, u32[]{:S(2)}) copy-start(bf16[2,24,24,128]{3,2,1,0:T(8,128)(2,1)} %param.5) | copy-start | bytes 884740
  2.6 1.0 %copy-start.1 = (bf16[24,24,256]{2,1,0:T(8,128)(2,1)S(1)}, bf16[24,24,256]{2,1,0:T(8,128)(2,1)}, u32[]{:S(2)}) copy-start(bf16[24,24,256]{2,1,0:T(8,128)(2,1)} %param.3) | copy-start | bytes 884740
